TPU v7x, 256 devices: a whole 4x4x8 slice. The times are simulated.
256 devices in a mesh: row: 8 (over x_lo, y), col: 32 (over z, x_hi, core).
Axes of the slice: x: 4 (x_hi: 2, x_lo: 2; x = x_hi * 2 + x_lo), y: 4, z: 8, core: 2. Of those that a mesh axis runs over, the one named last changes fastest.
Arguments:
- queries: bfloat16 [128, 256, 1024], P('row', 'col'), may hold values from -16 to 16
- keys: bfloat16 [128, 256, 1024], P('row', 'col'), may hold values from -16 to 16
- values: bfloat16 [128, 256, 1024], P('row', 'col'), may hold values from -6 to 6
- grad_out: bfloat16 [128, 256, 1024], P('row', 'col'), may hold values from -190 to 190
- out_weight: bfloat16 [1024, 1024], replicated, may hold values from -0.1875 to 0.1875
- rel_bias: float32 [16, 121], replicated, may hold values from -4 to 4
Outputs:
- grad_queries: bfloat16 [128, 256, 1024], P('row', 'col')
- grad_keys: bfloat16 [128, 256, 1024], P('row', 'col')
- grad_values: bfloat16 [128, 256, 1024], P('row', 'col')
- grad_out_weight: bfloat16 [1024, 1024], replicated
- grad_bias: float32 [16, 121], replicated
All inputs are finite; a program needn't handle non-finite values.
Results may differ from a plain program's by a relative error of at most 0.0068.
Values may be sent and summed in bfloat16 or wider, within the bound.
A program may use at most 128 MiB of HBM per device.

v0:
```python
import math

import jax
import jax.numpy as jnp
import numpy as np
from jax import lax
from jax.sharding import PartitionSpec as P

RAD = 5
KS = 11


def passed_along(block, axis, distance):
    devices = range(lax.axis_size(axis))
    route = [(i - distance, i) for i in devices if i - distance in devices]
    return lax.ppermute(block, axis, route)


def with_halo(cells, sides, width):
    for axis, dim in sides:
        count = lax.axis_size(axis)
        ends = count - 1
        head = lax.slice_in_dim(cells, 0, width, axis=dim)
        tail = lax.slice_in_dim(cells, cells.shape[dim] - width, cells.shape[dim], axis=dim)
        cells = jnp.concatenate(
            [
                lax.ppermute(tail, axis, [(i, (i + 1) % count) for i in range(ends)]),
                cells,
                lax.ppermute(head, axis, [((i + 1) % count, i) for i in range(ends)]),
            ],
            axis=dim,
        )
    return cells


def offset_table(query_rows, query_cols, radius):
    window_side = 2 * radius + 1
    key_rows = query_rows + 2 * radius
    key_cols = query_cols + 2 * radius
    query_row = np.repeat(np.arange(query_rows), query_cols)
    query_col = np.tile(np.arange(query_cols), query_rows)
    key_row = np.repeat(np.arange(key_rows), key_cols)
    key_col = np.tile(np.arange(key_cols), key_rows)
    row_step = key_row[None, :] - radius - query_row[:, None]
    col_step = key_col[None, :] - radius - query_col[:, None]
    inside = (np.abs(row_step) <= radius) & (np.abs(col_step) <= radius)
    offsets = np.where(
        inside, (row_step + radius) * window_side + col_step + radius, window_side * window_side
    )
    return (offsets.astype(np.int32), inside)


def key_block_mask(first_row, first_col, key_rows, key_cols, total_rows, total_cols):
    rows_global = first_row + jnp.arange(key_rows, dtype=jnp.int32)
    cols_global = first_col + jnp.arange(key_cols, dtype=jnp.int32)
    inside_rows = (rows_global >= 0) & (rows_global < total_rows)
    inside_cols = (cols_global >= 0) & (cols_global < total_cols)
    return (inside_rows[:, None] & inside_cols[None, :]).reshape(-1)


def skew_diagonals(plane, window_side):
    lead = plane.shape[:-2]
    outer = plane.shape[-2]
    inner = plane.shape[-1]
    flat = plane.reshape(lead + (outer * inner,))
    widths = [(0, 0)] * len(lead) + [(0, outer)]
    flat = jnp.pad(flat, widths)
    shaped = flat.reshape(lead + (outer, inner + 1))
    return jnp.sum(shaped[..., :window_side], axis=-2)


def fold_window(score_total, query_rows, query_cols, key_rows, key_cols, window_side):
    head_count = score_total.shape[0]
    grid = score_total.reshape(head_count, query_rows, query_cols, key_rows, key_cols)
    by_rows = jnp.transpose(grid, (0, 2, 4, 1, 3))
    row_folded = skew_diagonals(by_rows, window_side)
    by_cols = jnp.transpose(row_folded, (0, 3, 1, 2))
    col_folded = skew_diagonals(by_cols, window_side)
    return col_folded.reshape(head_count, window_side * window_side)


def attend_block(queries, keys, values, grad_attn, bias_rows, allowed, score_scale):
    wide = jnp.float32
    scores = (
        jnp.einsum("qhd,khd->hqk", queries, keys, preferred_element_type=wide) * score_scale
        + bias_rows
    )
    scores = jnp.where(allowed[None], scores, -1e30)
    highest = jnp.max(scores, axis=-1, keepdims=True)
    weights = jnp.where(allowed[None], jnp.exp(scores - highest), 0.0)
    probabilities = weights / jnp.sum(weights, axis=-1, keepdims=True)
    probs_low = probabilities.astype(jnp.bfloat16)
    attended = jnp.einsum("hqk,khd->qhd", probs_low, values, preferred_element_type=wide).astype(
        jnp.bfloat16
    )
    prob_grad = jnp.einsum("qhd,khd->hqk", grad_attn, values, preferred_element_type=wide)
    center = jnp.sum(probabilities * prob_grad, axis=-1, keepdims=True)
    score_grad = probabilities * (prob_grad - center)
    score_low = score_grad.astype(jnp.bfloat16)
    grad_query = (
        jnp.einsum("hqk,khd->qhd", score_low, keys, preferred_element_type=wide) * score_scale
    ).astype(jnp.bfloat16)
    key_part = (
        jnp.einsum("hqk,qhd->khd", score_low, queries, preferred_element_type=wide) * score_scale
    )
    value_part = jnp.einsum("hqk,qhd->khd", probs_low, grad_attn, preferred_element_type=wide)
    return (attended, grad_query, key_part, value_part, score_grad)


def return_rims(grad_ext):
    left_rim = grad_ext[:, :, :RAD]
    right_rim = grad_ext[:, :, -RAD:]
    from_next = passed_along(left_rim, "col", -1)
    from_prev = passed_along(right_rim, "col", 1)
    middle = grad_ext[:, :, RAD:-RAD]
    column_count = middle.shape[2]
    middle = middle.at[:, :, :RAD].add(from_prev).at[:, :, column_count - RAD :].add(from_next)
    top_rim = middle[:, :RAD]
    bottom_rim = middle[:, -RAD:]
    from_below = passed_along(top_rim, "row", -1)
    from_above = passed_along(bottom_rim.astype(jnp.bfloat16), "row", 1).astype(bottom_rim.dtype)
    interior = middle[:, RAD:-RAD]
    row_count = interior.shape[1]
    return interior.at[:, :RAD].add(from_above).at[:, row_count - RAD :].add(from_below)


def on_device(queries, keys, values, grad_out, out_weight, rel_bias):
    rows_dev, cols_dev, model_width = queries.shape
    head_count = rel_bias.shape[0]
    head_size = model_width // head_count
    score_scale = 1.0 / math.sqrt(head_size)
    half_rows = rows_dev // 2
    key_rows = half_rows + 2 * RAD
    key_cols = cols_dev + 2 * RAD
    group_size = min(8, head_count)
    kv_pair = jnp.stack([keys, values])
    extended = with_halo(kv_pair, (("row", 1), ("col", 2)), RAD)
    grad_flat = grad_out.reshape(-1, model_width)
    grad_attn = lax.dot_general(
        grad_flat, out_weight, (((1,), (1,)), ((), ())), preferred_element_type=jnp.float32
    )
    grad_attn = grad_attn.astype(jnp.bfloat16).reshape(rows_dev, cols_dev, model_width)
    offsets, inside = offset_table(half_rows, cols_dev, RAD)
    clipped = np.minimum(offsets, KS * KS - 1)
    inside_mask = jnp.asarray(inside)
    bias_table = rel_bias[:, clipped]
    total_rows = rows_dev * lax.axis_size("row")
    total_cols = cols_dev * lax.axis_size("col")
    top_row = lax.axis_index("row") * rows_dev - RAD
    left_col = lax.axis_index("col") * cols_dev - RAD
    grad_ext = jnp.zeros((2, rows_dev + 2 * RAD, key_cols, model_width), jnp.float32)
    score_total = jnp.zeros((head_count, half_rows * cols_dev, key_rows * key_cols), jnp.float32)
    attended_rows = []
    query_rows = []
    for block_index in range(2):
        first = block_index * half_rows
        key_slab = extended[:, first : first + key_rows].reshape(
            2, key_rows * key_cols, head_count, head_size
        )
        query_block = queries[first : first + half_rows].reshape(-1, head_count, head_size)
        grad_block = grad_attn[first : first + half_rows].reshape(-1, head_count, head_size)
        allowed = (
            inside_mask
            & key_block_mask(top_row + first, left_col, key_rows, key_cols, total_rows, total_cols)[
                None, :
            ]
        )
        attended_heads = []
        query_heads = []
        key_heads = []
        value_heads = []
        score_heads = []
        for first_head in range(0, head_count, group_size):
            last_head = first_head + group_size
            results = attend_block(
                query_block[:, first_head:last_head],
                key_slab[0][:, first_head:last_head],
                key_slab[1][:, first_head:last_head],
                grad_block[:, first_head:last_head],
                bias_table[first_head:last_head],
                allowed,
                score_scale,
            )
            attended_heads.append(results[0])
            query_heads.append(results[1])
            key_heads.append(results[2])
            value_heads.append(results[3])
            score_heads.append(results[4])
        score_total = score_total + jnp.concatenate(score_heads, axis=0)
        key_sum = jnp.concatenate(key_heads, axis=1).reshape(key_rows, key_cols, model_width)
        value_sum = jnp.concatenate(value_heads, axis=1).reshape(key_rows, key_cols, model_width)
        grad_ext = grad_ext.at[0, first : first + key_rows].add(key_sum)
        grad_ext = grad_ext.at[1, first : first + key_rows].add(value_sum)
        attended_rows.append(
            jnp.concatenate(attended_heads, axis=1).reshape(half_rows, cols_dev, model_width)
        )
        query_rows.append(
            jnp.concatenate(query_heads, axis=1).reshape(half_rows, cols_dev, model_width)
        )
    bias_grad = fold_window(score_total, half_rows, cols_dev, key_rows, key_cols, KS)
    attended = jnp.concatenate(attended_rows, axis=0)
    grad_queries = jnp.concatenate(query_rows, axis=0)
    returned = return_rims(grad_ext)
    grad_keys = returned[0].astype(jnp.bfloat16)
    grad_values = returned[1].astype(jnp.bfloat16)
    attended_flat = attended.reshape(-1, model_width)
    weight_term = lax.dot_general(
        attended_flat, grad_flat, (((0,), (0,)), ((), ())), preferred_element_type=jnp.float32
    )
    summed, bias_total = lax.psum((weight_term, bias_grad), ("row", "col"))
    grad_out_weight = summed.astype(jnp.bfloat16)
    return (grad_queries, grad_keys, grad_values, grad_out_weight, bias_total)


def solution(mesh):
    placed = (
        P("row", "col", None),
        P("row", "col", None),
        P("row", "col", None),
        P("row", "col", None),
        P(),
        P(),
    )
    return jax.shard_map(
        on_device,
        mesh=mesh,
        in_specs=placed,
        out_specs=(P("row", "col", None), P("row", "col", None), P("row", "col", None), P(), P()),
        check_vma=False,
    )
```

profile of v0, /device:TPU:7, one launch (start us, length us, event | category | flops | bytes accessed | tf_op | source)
XLA Modules:
  0.0 478.2 jit_solution(2268373811796320844)
XLA Ops:
  2.6 3.2 collective-permute-start
  5.8 4.2 collective-permute-start.1
  17.5 38.8 %gather_fusion = f32[20736,16]{1,0:T(8,128)} fusion(f32[16,121]{0,1:T(8,128)S(1)} %copy.129, s32[21504]{0:T(1024)S(1)} %pad_clamp_fusion), kind=kCustom, calls=%fused_computation | custom fusion | bytes 2737152 | tf_op jit(solution)/shard_map/gather | solution.py:146
  56.3 6.2 %copy.130 = f32[20736,16]{0,1:T(8,128)S(1)} copy(f32[20736,16]{1,0:T(8,128)} %gather_fusion) | data formatting | bytes 2654208 | tf_op jit(solution)/shard_map/gather | solution.py:146
  67.8 3.1 collective-permute-start.3
  71.0 4.8 %collective-permute-start.2 = (bf16[2,26,5,1024]{3,0,2,1:T(2,128)(2,1)S(1)}, bf16[2,26,5,1024]{3,0,2,1:T(2,128)(2,1)S(1)}, u32[]{:S(2)}, u32[]{:S(2)}) collective-permute-start(bf16[2,26,5,1024]{3,0,2,1:T(2,128)(2,1)S(1)} %copy.123), channel_id=1, source_target_pairs={{0,1},{1,2},{2,3},{3,4},{4,5},{5,6},{6,7},{7,8},{8,9},{9,10},{10,1... | collective-permute-start | bytes 1597448 | tf_op jit(solution)/shard_map/ppermute | solution.py:27
  77.8 3.1 collective-permute-done.3
  82.3 2.6 pad_maximum_fusion
  84.8 2.0 fusion.92
  86.8 2.0 squeeze.21
  90.0 2.2 copy.190
  92.2 2.0 squeeze.20
  98.3 2.7 fusion.41
  101.0 2.0 convolution_bitcast_fusion.2
  106.2 3.5 concatenate.89
  109.7 2.3 copy.194
  115.7 3.3 fusion.42
  119.0 3.4 convolution_bitcast_fusion.1
  126.4 4.8 %concatenate.90 = f32[8,8,8,18,18]{4,3,2,1,0:T(8,128)} reshape(f32[8,64,324]{2,1,0:T(8,128)} %copy-done.3) | data formatting | bytes 1327104 | tf_op jit(solution)/shard_map/concatenate | solution.py:189
  131.1 2.8 squeeze.9
  134.0 2.4 fusion.94
  136.4 2.2 copy.182
  138.6 3.2 squeeze.8
  141.8 2.5 fusion.95
  148.1 3.2 fusion.39
  151.4 3.4 convolution_bitcast_fusion.4
  158.8 4.7 concatenate.86
  163.5 2.2 copy.186
  168.7 3.4 fusion.40
  172.1 3.4 convolution_bitcast_fusion.3
  177.2 3.5 concatenate.87
  183.5 2.2 copy.155
  185.8 2.2 reshape.455
  187.9 2.7 pad_maximum_fusion.4
  190.6 3.3 copy.158
  193.9 3.1 reshape.456
  197.0 2.7 pad_maximum_fusion.1
  199.6 3.3 copy.149
  202.9 3.2 add.140
  206.1 2.7 pad_maximum_fusion.2
  208.8 3.3 copy.152
  212.0 3.1 add.141
  215.1 2.2 scatter-add.26
  217.6 2.4 fusion.5
  225.8 7.1 %collective-permute-start.4 = (f32[2,26,5,1024]{3,0,2,1:T(2,128)}, f32[2,26,5,1024]{3,0,2,1:T(2,128)}, u32[]{:S(2)}, u32[]{:S(2)}) collective-permute-start(f32[2,26,5,1024]{3,0,2,1:T(2,128)} %copy.159), channel_id=1, source_target_pairs={{0,1},{1,2},{2,3},{3,4},{4,5},{5,6},{6,7},{7,8},{8,9},{9,10},{10,1... | collective-permute-start | bytes 3194888 | tf_op jit(solution)/shard_map/ppermute | solution.py:16
  232.9 2.7 convolution_bitcast_fusion
  235.6 8.9 %fusion.4 = f32[16,8,18,8,18]{2,4,1,3,0:T(8,128)} fusion(f32[8,8,8,18,18]{4,3,2,1,0:T(8,128)} %concatenate.87, f32[8,8,8,18,18]{4,3,2,1,0:T(8,128)S(1)} %bitcast.123, f32[8,8,8,18,18]{4,3,2,1,0:T(8,128)S(1)} %bitcast.121, f32[8,8,8,18,18]{4,3,2,1,0:T(8,128)S(1)} %bitcast.119), kind=kLoop, calls=%fused_computation.6 | loop fusion | flops 995328 | bytes 3981312 | tf_op jit(solution)/shard_map/transpose | solution.py:75
  244.5 13.9 %copy.168 = f32[16,8,18,8,18]{4,3,1,2,0:T(8,128)} copy(f32[16,8,18,8,18]{2,4,1,3,0:T(8,128)} %fusion.4) | data formatting | bytes 2654208 | tf_op jit(solution)/shard_map/transpose | solution.py:75
  258.4 7.4 %reshape.459 = f32[16,8,18,144]{3,1,2,0:T(8,128)} reshape(f32[16,8,18,8,18]{4,3,1,2,0:T(8,128)} %copy.168) | data formatting | bytes 2654208 | tf_op jit(solution)/shard_map/reshape | solution.py:65
  265.8 3.2 pad.33
  269.0 7.2 %reshape.460 = f32[16,8,18,8,19]{4,3,1,2,0:T(8,128)} reshape(f32[16,8,18,152]{3,1,2,0:T(8,128)} %pad.33) | data formatting | bytes 2801664 | tf_op jit(solution)/shard_map/reshape | solution.py:68
  276.3 6.7 %slice_reduce_fusion = f32[16,8,18,11]{3,1,2,0:T(8,128)S(1)} fusion(f32[16,8,18,8,19]{4,3,1,2,0:T(8,128)} %reshape.460), kind=kLoop, calls=%fused_computation.7 | loop fusion | flops 177408 | bytes 912384 | tf_op jit(solution)/shard_map/reduce_sum | solution.py:69
  284.8 135.6 %all-reduce.5 = (bf16[1024,1024]{1,0:T(8,128)(2,1)}, f32[16,121]{1,0:T(8,128)}) all-reduce(f32[1024,1024]{1,0:T(8,128)} %convolution_bitcast_fusion, f32[16,121]{1,0:T(8,128)S(1)} %reshape.463), channel_id=1, replica_groups=mesh['row'=8,'col'=32] {'row','col'}, use_global_device_ids=true, to_apply=%region_13.14 | all-reduce | flops 1050512 | bytes 6306944 | tf_op jit(solution)/shard_map/psum | solution.py:210
  420.4 2.6 slice.461
  424.9 2.1 collective-permute-start.5
  428.6 4.1 slice_add_fusion.2
  432.7 8.9 %scatter-add.34 = f32[2,26,8,1024]{3,2,1,0:T(8,128)S(1)} dynamic-update-slice(f32[2,26,8,1024]{3,2,1,0:T(8,128)S(1)} %slice.461, f32[2,26,5,1024]{3,2,1,0:T(8,128)} %slice_add_fusion.2, s32[]{:T(128)} %constant.253.clone.1, s32[]{:T(128)} %constant.253.clone.1, s32[]{:T(128)} %constant.253.clone.1, s32[]{:T(128)} %constant.253.clone.1) | dynamic-update-slice | bytes 2129924 | tf_op jit(solution)/shard_map/scatter-add | solution.py:117
  441.6 2.3 collective-permute-done.5
  443.9 3.0 slice_add_fusion.1
  446.9 8.9 %scatter-add.35 = f32[2,26,8,1024]{3,2,1,0:T(8,128)S(1)} dynamic-update-slice(f32[2,26,8,1024]{3,2,1,0:T(8,128)S(1)} %scatter-add.34, f32[2,26,5,1024]{3,2,1,0:T(8,128)} %slice_add_fusion.1, s32[]{:T(128)} %constant.253.clone.1, s32[]{:T(128)} %constant.253.clone.1, s32[]{:T(128)} %constant.263.clone.1, s32[]{:T(128)} %constant.253.clone.1) | dynamic-update-slice | bytes 2129924 | tf_op jit(solution)/shard_map/scatter-add | solution.py:117
  455.8 1.9 collective-permute-start.6
  458.1 6.0 %collective-permute-done.6 = bf16[2,5,8,1024]{3,2,1,0:T(8,128)(2,1)S(1)} collective-permute-done((bf16[2,5,8,1024]{3,2,1,0:T(8,128)(2,1)S(1)}, bf16[2,5,8,1024]{3,2,1,0:T(8,128)(2,1)S(1)}, u32[]{:S(2)}, u32[]{:S(2)}) %collective-permute-start.6) | collective-permute-done | bytes 163872 | tf_op jit(solution)/shard_map/ppermute | solution.py:16
  464.9 1.9 collective-permute-start.7
  470.2 5.8 %collective-permute-done.7 = f32[2,5,8,1024]{3,2,1,0:T(8,128)} collective-permute-done((f32[2,5,8,1024]{3,2,1,0:T(8,128)}, f32[2,5,8,1024]{3,2,1,0:T(8,128)}, u32[]{:S(2)}, u32[]{:S(2)}) %collective-permute-start.7) | collective-permute-done | bytes 327712 | tf_op jit(solution)/shard_map/ppermute | solution.py:16
  (211 shorter events, 66.4 us)
Async XLA Ops:
  0.6 10.6 %copy-start = (bf16[1024,1024]{1,0:T(8,128)(2,1)S(1)}, bf16[1024,1024]{1,0:T(8,128)(2,1)}, u32[]{:S(2)}) copy-start(bf16[1024,1024]{1,0:T(8,128)(2,1)} %param.29) | copy-start | bytes 6291460
  2.6 62.5 %collective-permute-start = (bf16[2,5,8,1024]{3,2,1,0:T(8,128)(2,1)}, bf16[2,5,8,1024]{3,2,1,0:T(8,128)(2,1)}, u32[]{:S(2)}, u32[]{:S(2)}) collective-permute-start(bf16[2,5,8,1024]{3,2,1,0:T(8,128)(2,1)} %get-tuple-element.123), channel_id=1, source_target_pairs={{0,32},{32,64},{64,96},{96,128},{128,160},{160,192},{192,224},{1,3... | collective-permute-start | bytes 491528 | tf_op jit(solution)/shard_map/ppermute | solution.py:27
  5.8 59.3 %collective-permute-start.1 = (bf16[2,5,8,1024]{3,2,1,0:T(8,128)(2,1)}, bf16[2,5,8,1024]{3,2,1,0:T(8,128)(2,1)}, u32[]{:S(2)}, u32[]{:S(2)}) collective-permute-start(bf16[2,5,8,1024]{3,2,1,0:T(8,128)(2,1)} %get-tuple-element.124), channel_id=1, source_target_pairs={{32,0},{64,32},{96,64},{128,96},{160,128},{192,160},{224,192},{33,... | collective-permute-start | bytes 491528 | tf_op jit(solution)/shard_map/ppermute | solution.py:29
  11.2 3.7 copy-start.39
  13.0 1.9 copy-start.46
  13.0 2.6 copy-start.47
  62.5 1.8 copy-start.48
  62.5 2.6 copy-start.24
  62.5 2.5 copy-start.25
  66.6 9.8 %copy-start.30 = (bf16[64,16,64]{2,1,0:T(8,128)(2,1)S(1)}, bf16[64,16,64]{2,1,0:T(8,128)(2,1)}, u32[]{:S(2)}) copy-start(bf16[64,16,64]{2,1,0:T(8,128)(2,1)} %reshape.446) | copy-start | bytes 393220
  66.6 10.5 %copy-start.29 = (bf16[64,16,64]{2,1,0:T(8,128)(2,1)S(1)}, bf16[64,16,64]{2,1,0:T(8,128)(2,1)}, u32[]{:S(2)}) copy-start(bf16[64,16,64]{2,1,0:T(8,128)(2,1)} %reshape.450) | copy-start | bytes 393220
  67.8 13.1 %collective-permute-start.3 = (bf16[2,26,5,1024]{3,0,2,1:T(2,128)(2,1)S(1)}, bf16[2,26,5,1024]{3,0,2,1:T(2,128)(2,1)S(1)}, u32[]{:S(2)}, u32[]{:S(2)}) collective-permute-start(bf16[2,26,5,1024]{3,0,2,1:T(2,128)(2,1)S(1)} %copy.124), channel_id=1, source_target_pairs={{1,0},{2,1},{3,2},{4,3},{5,4},{6,5},{7,6},{8,7},{9,8},{10,9},{11,1... | collective-permute-start | bytes 1597448 | tf_op jit(solution)/shard_map/ppermute | solution.py:29
  71.0 11.1 %collective-permute-start.2 = (bf16[2,26,5,1024]{3,0,2,1:T(2,128)(2,1)S(1)}, bf16[2,26,5,1024]{3,0,2,1:T(2,128)(2,1)S(1)}, u32[]{:S(2)}, u32[]{:S(2)}) collective-permute-start(bf16[2,26,5,1024]{3,0,2,1:T(2,128)(2,1)S(1)} %copy.123), channel_id=1, source_target_pairs={{0,1},{1,2},{2,3},{3,4},{4,5},{5,6},{6,7},{7,8},{8,9},{9,10},{10,1... | collective-permute-start | bytes 1597448 | tf_op jit(solution)/shard_map/ppermute | solution.py:27
  94.2 2.7 copy-start.28
  94.2 2.7 copy-start.32
  98.3 2.8 copy-start.42
  103.0 1.7 copy-start.22
  109.7 3.8 copy-start.27
  109.7 3.8 copy-start.33
  113.4 5.6 %copy-start.12 = (bf16[324,8,64]{0,2,1:T(8,128)(2,1)}, bf16[324,8,64]{0,2,1:T(8,128)(2,1)S(1)}, u32[]{:S(2)}) copy-start(bf16[324,8,64]{0,2,1:T(8,128)(2,1)S(1)} %copy.191) | copy-start | bytes 995332
  113.7 0.9 copy-start.19
  119.0 3.4 copy-start.37
  122.4 1.6 copy-start.21
  124.3 0.9 copy-start.3
  141.8 4.1 copy-start.26
  141.8 4.0 copy-start.31
  145.9 5.5 %copy-start.14 = (bf16[324,8,64]{0,2,1:T(8,128)(2,1)}, bf16[324,8,64]{0,2,1:T(8,128)(2,1)S(1)}, u32[]{:S(2)}) copy-start(bf16[324,8,64]{0,2,1:T(8,128)(2,1)S(1)} %copy.179) | copy-start | bytes 995332
  146.1 0.9 copy-start.20
  151.4 3.4 copy-start.35
  154.8 1.6 copy-start.23
  156.6 0.9 copy-start.5
  167.2 4.8 %copy-start.16 = (bf16[324,8,64]{0,2,1:T(8,128)(2,1)}, bf16[324,8,64]{0,2,1:T(8,128)(2,1)S(1)}, u32[]{:S(2)}) copy-start(bf16[324,8,64]{0,2,1:T(8,128)(2,1)S(1)} %copy.183) | copy-start | bytes 995332
  167.5 0.9 copy-start.18
  168.7 3.4 copy-start.40
  172.0 3.4 copy-start.36
  176.0 4.8 copy-start.7
  177.2 3.5 copy-start.44
  177.2 3.5 copy-start.45
  177.2 4.1 copy-start.41
  177.2 4.2 copy-start.43
  215.1 2.2 copy-start.9
  217.6 2.4 copy-start.10
  220.0 15.6 %slice-start.4 = ((s8[6291456]{0:T(1024)(128)(4,1)}), s8[4194304]{0:T(1024)(128)(4,1)S(1)}, s32[]{:S(2)}) async-start(s8[6291456]{0:T(1024)(128)(4,1)} %bitcast.122), calls=%async_computation.4 | async-start | bytes 8388608
  220.5 3.4 copy-start.2
  220.5 15.0 %slice-start.2 = ((s8[6291456]{0:T(1024)(128)(4,1)}), s8[4194304]{0:T(1024)(128)(4,1)S(1)}, s32[]{:S(2)}) async-start(s8[6291456]{0:T(1024)(128)(4,1)} %bitcast.120), calls=%async_computation.2 | async-start | bytes 8388608
  223.9 8.9 %copy-start.38 = (bf16[16,8,1024]{2,1,0:T(8,128)(2,1)S(1)}, bf16[16,8,1024]{2,1,0:T(8,128)(2,1)}, u32[]{:S(2)}) copy-start(bf16[16,8,1024]{2,1,0:T(8,128)(2,1)} %param.28) | copy-start | bytes 786436
  223.9 11.6 %slice-start = ((s8[6291456]{0:T(1024)(128)(4,1)}), s8[4194304]{0:T(1024)(128)(4,1)S(1)}, s32[]{:S(2)}) async-start(s8[6291456]{0:T(1024)(128)(4,1)} %bitcast.118), calls=%async_computation | async-start | bytes 8388608
  223.9 11.6 %slice-start.5 = ((s8[6291456]{0:T(1024)(128)(4,1)}), s8[2097152]{0:T(1024)(128)(4,1)S(1)}, s32[]{:S(2)}) async-start(s8[6291456]{0:T(1024)(128)(4,1)} %bitcast.122), calls=%async_computation.5 | async-start | bytes 4194304
  225.8 9.8 %slice-start.1 = ((s8[6291456]{0:T(1024)(128)(4,1)}), s8[2097152]{0:T(1024)(128)(4,1)S(1)}, s32[]{:S(2)}) async-start(s8[6291456]{0:T(1024)(128)(4,1)} %bitcast.118), calls=%async_computation.1 | async-start | bytes 4194304
  225.8 9.9 %slice-start.3 = ((s8[6291456]{0:T(1024)(128)(4,1)}), s8[2097152]{0:T(1024)(128)(4,1)S(1)}, s32[]{:S(2)}) async-start(s8[6291456]{0:T(1024)(128)(4,1)} %bitcast.120), calls=%async_computation.3 | async-start | bytes 4194304
  225.8 202.8 %collective-permute-start.4 = (f32[2,26,5,1024]{3,0,2,1:T(2,128)}, f32[2,26,5,1024]{3,0,2,1:T(2,128)}, u32[]{:S(2)}, u32[]{:S(2)}) collective-permute-start(f32[2,26,5,1024]{3,0,2,1:T(2,128)} %copy.159), channel_id=1, source_target_pairs={{0,1},{1,2},{2,3},{3,4},{4,5},{5,6},{6,7},{7,8},{8,9},{9,10},{10,1... | collective-permute-start | bytes 3194888 | tf_op jit(solution)/shard_map/ppermute | solution.py:16
  420.4 2.6 copy-start.11
  423.0 4.0 copy-start.8
  423.0 4.0 copy-start.17
  423.0 4.3 copy-start.6
  423.0 4.3 copy-start.15
  423.0 5.2 %copy-start.4 = (f32[8,64,324]{2,1,0:T(8,128)S(1)}, f32[8,64,324]{2,1,0:T(8,128)}, u32[]{:S(2)}) copy-start(f32[8,64,324]{2,1,0:T(8,128)} %copy-done.3) | copy-start | bytes 1990660
  423.1 5.2 %copy-start.13 = (bf16[324,8,64]{0,2,1:T(8,128)(2,1)S(1)}, bf16[324,8,64]{0,2,1:T(8,128)(2,1)}, u32[]{:S(2)}) copy-start(bf16[324,8,64]{0,2,1:T(8,128)(2,1)} %copy-done.12) | copy-start | bytes 995332
  424.9 19.0 %collective-permute-start.5 = (f32[2,26,5,1024]{3,0,2,1:T(2,128)}, f32[2,26,5,1024]{3,0,2,1:T(2,128)}, u32[]{:S(2)}, u32[]{:S(2)}) collective-permute-start(f32[2,26,5,1024]{3,0,2,1:T(2,128)} %copy.161), channel_id=1, source_target_pairs={{1,0},{2,1},{3,2},{4,3},{5,4},{6,5},{7,6},{8,7},{9,8},{10,9},{11,1... | collective-permute-start | bytes 3194888 | tf_op jit(solution)/shard_map/ppermute | solution.py:16
  455.8 8.3 %collective-permute-start.6 = (bf16[2,5,8,1024]{3,2,1,0:T(8,128)(2,1)S(1)}, bf16[2,5,8,1024]{3,2,1,0:T(8,128)(2,1)S(1)}, u32[]{:S(2)}, u32[]{:S(2)}) collective-permute-start(bf16[2,5,8,1024]{3,2,1,0:T(8,128)(2,1)S(1)} %slice.495), channel_id=1, source_target_pairs={{0,32},{32,64},{64,96},{96,128},{128,160},{160,192},{192,224},{1,3... | collective-permute-start | bytes 491528 | tf_op jit(solution)/shard_map/ppermute | solution.py:16
  458.0 8.8 %copy-start.34 = (bf16[64,8,64]{0,2,1:T(8,128)(2,1)S(1)}, bf16[64,8,64]{0,2,1:T(8,128)(2,1)}, u32[]{:S(2)}) copy-start(bf16[64,8,64]{0,2,1:T(8,128)(2,1)} %fusion.46) | copy-start | bytes 196612
  464.9 11.1 %collective-permute-start.7 = (f32[2,5,8,1024]{3,2,1,0:T(8,128)}, f32[2,5,8,1024]{3,2,1,0:T(8,128)}, u32[]{:S(2)}, u32[]{:S(2)}) collective-permute-start(f32[2,5,8,1024]{3,2,1,0:T(8,128)} %get-tuple-element.109), channel_id=1, source_target_pairs={{32,0},{64,32},{96,64},{128,96},{160,128},{192,160},{224,192},{33,... | collective-permute-start | bytes 983048 | tf_op jit(solution)/shard_map/ppermute | solution.py:16
  467.7 10.3 %copy-start.1 = (bf16[1024,1024]{1,0:T(8,128)(2,1)S(1)}, bf16[1024,1024]{1,0:T(8,128)(2,1)}, u32[]{:S(2)}) copy-start(bf16[1024,1024]{1,0:T(8,128)(2,1)} %param.29) | copy-start | bytes 6291460
where the time goes:
time: 486 us; the launch traced here: 478 us
  local copies, waits for them, and re-layouts  200 us (41%)
  blocking collectives  136 us (28%)
  other arithmetic  51.5 us (11%)
  matrix products  42.3 us (9%)
  starting transfers between devices  28.4 us (6%)
  waiting for transfers between devices  18.2 us (4%)
    psum x1, blocking collectives, on_device(): summed, bias_total = lax.psum((weight_term, bias_grad), ('row', 'col'))  136 us
    gather x3, local copies, waits for them, and re-layouts, on_device(): bias_table = rel_bias[:, clipped]  46.7 us
    unnamed x119, local copies, waits for them, and re-layouts  21.3 us
    scatter-add x2, local copies, waits for them, and re-layouts, return_rims(): middle.at[:, :, :RAD].add(from_prev).at[:, :, column_count - RAD:]  17.7 us
    concatenate x4, local copies, waits for them, and re-layouts, on_device(): score_total = score_total + jnp.concatenate(score_heads, axis=0)  16.5 us
    ppermute x4, waiting for transfers between devices, passed_along(): return lax.ppermute(block, axis, route)  14.2 us
    transpose x1, local copies, waits for them, and re-layouts, fold_window(): by_rows = jnp.transpose(grid, (0, 2, 4, 1, 3))  13.9 us
    ppermute x4, starting transfers between devices, passed_along(): return lax.ppermute(block, axis, route)  13 us
  transfers between devices with their start and end apart: 8, of which 5 were waited for; matrix products, arithmetic and copies ran while one was open for 27% of the time, Pallas kernels for 0%

commit v1 on v0

v1 whole, which is shorter than its diff:
```python
import functools
import math

import jax
import jax.numpy as jnp
import numpy as np
from jax import lax
from jax.experimental import pallas as pl
from jax.experimental.pallas import tpu as pltpu
from jax.sharding import PartitionSpec as P

MESH = pl.DeviceIdType.MESH
BF = jnp.bfloat16
F32 = jnp.float32

RAD = 5
KS = 11
D = 1024
HEADS = 16
CH = 16
CW = 8
CELLS = CH * CW
XLO, NY, NZ, XHI, CORES = 2, 4, 8, 2, 2
NX = XLO * XHI
GROUP = NY * CORES
RING = NX * NZ
BLOCKS = 4
BROWS = CH // BLOCKS
BQ = BROWS * CW
MIDK = (BROWS + 2 * RAD) * CW
SIDEK = 72
KEYS = MIDK + 2 * SIDEK
STAGE = 144
EXT = CH + 2 * RAD
FEATS = D // NY
OUTS = D // CORES
PROWS = 16
PCOLS = 256
PIECES = FEATS // PROWS
NEG = -1e30
NEIGHBOURS = ((0, -1), (0, 1), (-1, 0), (1, 0), (-1, -1), (1, -1), (-1, 1), (1, 1))


def key_places():
    rows = np.full(KEYS, 1000, np.int64)
    cols = np.full(KEYS, 1000, np.int64)
    mid = np.arange(MIDK)
    rows[:MIDK], cols[:MIDK] = mid // CW, mid % CW
    side = np.arange(70)
    for first, base in ((MIDK, -RAD), (MIDK + SIDEK, CW)):
        rows[first + 1 : first + 71] = side // RAD
        cols[first + 1 : first + 71] = base + side % RAD
    return rows, cols


def tables():
    rows, cols = key_places()
    query = np.arange(BQ)
    dr = rows[None, :] - RAD - (query // CW)[:, None]
    dc = cols[None, :] - (query % CW)[:, None]
    inside = (np.abs(dr) <= RAD) & (np.abs(dc) <= RAD)
    offsets = np.where(inside, (dr + RAD) * KS + dc + RAD, 127)
    one_hot = offsets[:, :, None] == np.arange(128)[None, None, :]
    places = np.zeros((8, KEYS), np.int32)
    places[0], places[1] = rows, cols
    pack = np.zeros((2 * 80, CELLS), bool)
    edge = np.arange(80)
    pack[edge, edge // RAD * CW + edge % RAD] = True
    pack[80 + edge, edge // RAD * CW + CW - RAD + edge % RAD] = True
    spread = np.zeros((BLOCKS * SIDEK, STAGE), bool)
    for b in range(BLOCKS):
        place = np.arange(SIDEK)
        spread[b * SIDEK + place, 6 + 20 * b + place] = True
    entry = np.arange(STAGE)
    cell = np.where(entry < 32, entry, np.where(entry < 112, entry - 32, entry - 64))
    home = np.zeros((CELLS, 2 * STAGE), bool)
    home[cell // RAD * CW + cell % RAD, entry] = True
    home[cell // RAD * CW + CW - RAD + cell % RAD, STAGE + entry] = True
    heads = np.repeat(np.arange(4), BQ)[:, None] == (np.arange(256) // 64)[None, :]
    as_low = lambda t: np.asarray(t, np.float32).astype(jnp.bfloat16)
    return (as_low(one_hot), places, as_low(pack), as_low(spread), as_low(home), as_low(heads))


def dot(a, b, dims):
    return lax.dot_general(a, b, ((dims[0], dims[1]), ((), ())), preferred_element_type=F32)


NN = ((1,), (0,))
NT = ((1,), (1,))
TN = ((0,), (0,))


def kernel(
    q_hbm, k_hbm, v_hbm, g_hbm, w_hbm, bias_ref, oh_hbm, places_ref, pack_ref, spread_ref, home_ref, heads_ref,
    gq_ref, gk_ref, gv_ref, ow_hbm, ob_ref,
    qv, gv, wv, ohv, mid, panel_l, panel_r, stage_l, stage_r, ga, kb, vb, table, probs, att, att_t, at, go,
    sg_sum, acc_mid, acc_l, acc_r, ret_l, ret_r, rcv_l, rcv_r, up_out, down_out, up_in, down_in,
    wt, rs, out, bias_a, bias_ain, bias_xin, bias_b, bias_zin, bias_c, bias_d,
    loc_sem, halo_ss, halo_rs, go_ss, go_rs, at_ss, at_rs, ret_ss, ret_rs, rs_ss, rs_rs, ag_ss, ag_rs,
    y_ss, y_rs, c_ss, c_rs, ba_ss, ba_rs, bx_ss, bx_rs, bz_ss, bz_rs, bd_ss, bd_rs,
):
    row, col = lax.axis_index("row"), lax.axis_index("col")
    nrow, ncol = XLO * NY, NZ * XHI * CORES
    x = (col // CORES) % XHI * XLO + row // NY
    y, z, core = row % NY, col // (XHI * CORES), col % CORES
    scale = 1.0 / math.sqrt(D // HEADS)

    def device(x_at, y_at, z_at, core_at):
        return (x_at % XLO * NY + y_at, (z_at * XHI + x_at // XLO) * CORES + core_at)

    def neighbour(dr, dc):
        return ((row + dr + nrow) % nrow, (col + dc + ncol) % ncol)

    def member(k):
        yy = (y + k // CORES) % NY
        cc = (core + k % CORES) % CORES
        return yy, cc, device(x, yy, z, cc)

    def on_ring(k):
        xx = (x + k // NZ) % NX
        zz = (z + k % NZ) % NZ
        return xx * NZ + zz, device(xx, y, zz, core)

    me_group = y * CORES + core
    me_ring = x * NZ + z

    def local(src, dst, at_sem):
        return pltpu.make_async_copy(src, dst, loc_sem.at[at_sem])

    def remote(src, dst, ss, rsem, to):
        return pltpu.make_async_remote_copy(
            src_ref=src, dst_ref=dst, send_sem=ss, recv_sem=rsem, device_id=to, device_id_type=MESH
        )

    loads = [
        local(k_hbm, mid.at[0, RAD : RAD + CH], 0),
        local(v_hbm, mid.at[1, RAD : RAD + CH], 1),
        local(g_hbm, gv, 2),
        local(w_hbm, wv, 3),
        local(q_hbm, qv, 4),
        local(oh_hbm, ohv, 5),
    ]
    for c in loads:
        c.start()
    barrier = pltpu.get_barrier_semaphore()
    for dr, dc in NEIGHBOURS:
        pl.semaphore_signal(barrier, inc=1, device_id=neighbour(dr, dc), device_id_type=MESH)

    @pl.loop(1, GROUP)
    def _(k):
        pl.semaphore_signal(barrier, inc=1, device_id=member(k)[2], device_id_type=MESH)

    @pl.loop(1, RING)
    def _(k):
        pl.semaphore_signal(barrier, inc=1, device_id=on_ring(k)[1], device_id_type=MESH)

    loads[0].wait()
    loads[1].wait()
    for i in range(2):
        own = mid[i, RAD : RAD + CH].reshape(CELLS, D)
        packed = dot(pack_ref[...], own, NN).astype(BF)
        panel_l[i] = packed[:80]
        panel_r[i] = packed[80:]
    pl.semaphore_wait(barrier, len(NEIGHBOURS) + GROUP - 1 + RING - 1)

    halo_parts = (
        (panel_l, stage_r.at[:, 32:112]),
        (panel_r, stage_l.at[:, 32:112]),
        (mid.at[:, RAD : 2 * RAD], mid.at[:, RAD + CH :]),
        (mid.at[:, CH : CH + RAD], mid.at[:, :RAD]),
        (panel_l.at[:, 0:32], stage_r.at[:, 112:144]),
        (panel_l.at[:, 48:80], stage_r.at[:, 0:32]),
        (panel_r.at[:, 0:32], stage_l.at[:, 112:144]),
        (panel_r.at[:, 48:80], stage_l.at[:, 0:32]),
    )
    halo = [
        remote(src, dst, halo_ss.at[i], halo_rs.at[i], neighbour(*NEIGHBOURS[i]))
        for i, (src, dst) in enumerate(halo_parts)
    ]
    for c in halo:
        c.start()

    loads[2].wait()

    def go_copy(k):
        yy, cc, to = member(k)
        lanes = pl.ds(pl.multiple_of(cc * OUTS, OUTS), OUTS)
        return remote(gv.at[:, :, lanes], go.at[me_group], go_ss.at[k], go_rs.at[k], to)

    @pl.loop(1, GROUP)
    def _(k):
        go_copy(k).start()

    own_lanes = pl.ds(pl.multiple_of(core * OUTS, OUTS), OUTS)
    go_own = local(gv.at[:, :, own_lanes], go.at[me_group], 6)
    go_own.start()

    loads[3].wait()
    ga[...] = dot(gv[...].reshape(CELLS, D), wv[...], NT).astype(BF)

    loads[5].wait()
    padded = jnp.concatenate([bias_ref[...], jnp.full((HEADS, 128 - KS * KS), NEG, F32)], axis=1)
    high = padded.astype(BF)
    rest = padded - high.astype(F32)
    middle = rest.astype(BF)
    low = (rest - middle.astype(F32)).astype(BF)
    three = jnp.concatenate([high, middle, low], axis=0)
    for i in range(BQ):
        terms = dot(three, ohv[i], NT)
        table[:, i, :] = terms[:HEADS] + terms[HEADS : 2 * HEADS] + terms[2 * HEADS :]
    for ref in (acc_mid, acc_l, acc_r, sg_sum):
        ref[...] = jnp.zeros_like(ref)

    loads[4].wait()
    for c in halo:
        c.wait()
    for i, slab in enumerate((kb, vb)):
        left = dot(spread_ref[...], stage_l[i], NN)
        right = dot(spread_ref[...], stage_r[i], NN)
        for b in range(BLOCKS):
            slab[b, :MIDK] = mid[i, b * BROWS : b * BROWS + BROWS + 2 * RAD].reshape(MIDK, D)
            rows = slice(b * SIDEK, (b + 1) * SIDEK)
            slab[b, MIDK:] = jnp.concatenate([left[rows], right[rows]], axis=0).astype(BF)

    mask_low = heads_ref[...]
    mask_wide = mask_low.astype(F32)

    def spread_heads(tile):
        return jnp.concatenate([tile] * 4, axis=0) * mask_low

    def fold_heads(full):
        return jnp.sum((full * mask_wide).reshape(4, BQ, 256), axis=0)

    key_row, key_col = places_ref[0:1, :], places_ref[1:2, :]
    grid_col = col * CW + key_col
    col_ok = (grid_col >= 0) & (grid_col < ncol * CW)
    q2 = qv[...].reshape(CELLS, D)
    for b in range(BLOCKS):
        cells = slice(b * BQ, (b + 1) * BQ)
        grid_row = row * CH + b * BROWS - RAD + key_row
        present = col_ok & (grid_row >= 0) & (grid_row < nrow * CH)
        absent = jnp.where(present, 0.0, NEG)
        for h in range(4):
            lanes = slice(h * 256, (h + 1) * 256)
            qm = spread_heads(q2[cells, lanes])
            bias = table[4 * h : 4 * h + 4].reshape(4 * BQ, KEYS)
            scores = dot(qm, kb[b, :, lanes], NT) * scale + bias + absent
            weights = jnp.exp(scores - jnp.max(scores, axis=1, keepdims=True))
            p = weights * (1.0 / jnp.sum(weights, axis=1, keepdims=True))
            probs[b * 4 + h] = p
            att[cells, lanes] = fold_heads(dot(p.astype(BF), vb[b, :, lanes], NN)).astype(BF)
    att_t[...] = att[...].T

    def at_copy(k):
        yy, cc, to = member(k)
        src = att_t.at[pl.ds(pl.multiple_of(yy * FEATS, FEATS), FEATS)]
        dst = at.at[:, pl.ds(pl.multiple_of(me_group * CELLS, CELLS), CELLS)]
        return remote(src, dst, at_ss.at[k], at_rs.at[k], to)

    @pl.loop(1, GROUP)
    def _(k):
        at_copy(k).start()

    at_own = local(
        att_t.at[pl.ds(pl.multiple_of(y * FEATS, FEATS), FEATS)],
        at.at[:, pl.ds(pl.multiple_of(me_group * CELLS, CELLS), CELLS)],
        7,
    )
    at_own.start()

    for b in range(BLOCKS):
        cells = slice(b * BQ, (b + 1) * BQ)
        for h in range(4):
            lanes = slice(h * 256, (h + 1) * 256)
            qm = spread_heads(q2[cells, lanes])
            gm = spread_heads(ga[cells, lanes])
            p = probs[b * 4 + h]
            dp = dot(gm, vb[b, :, lanes], NT)
            sg = p * (dp - jnp.sum(p * dp, axis=1, keepdims=True))
            sg_sum[4 * h : 4 * h + 4] += sg.reshape(4, BQ, KEYS)
            sl = sg.astype(BF)
            gq_ref[cells, lanes] = (fold_heads(dot(sl, kb[b, :, lanes], NN)) * scale).astype(BF)
            parts = (dot(sl, qm, TN) * scale, dot(p.astype(BF), gm, TN))
            for i, part in enumerate(parts):
                acc_mid[i, b * BQ : b * BQ + MIDK, lanes] += part[:MIDK]
                acc_l[i, 6 + 20 * b : 6 + 20 * b + SIDEK, lanes] += part[MIDK : MIDK + SIDEK]
                acc_r[i, 6 + 20 * b : 6 + 20 * b + SIDEK, lanes] += part[MIDK + SIDEK :]

    ret_l[...] = acc_l[...].astype(BF)
    ret_r[...] = acc_r[...].astype(BF)
    up_out[...] = acc_mid[:, : RAD * CW].reshape(2, RAD, CW, D).astype(BF)
    down_out[...] = acc_mid[:, (RAD + CH) * CW :].reshape(2, RAD, CW, D).astype(BF)
    ret_parts = (
        (ret_l.at[:, 32:112], rcv_r.at[:, 32:112]),
        (ret_r.at[:, 32:112], rcv_l.at[:, 32:112]),
        (up_out, down_in),
        (down_out, up_in),
        (ret_l.at[:, 0:32], rcv_r.at[:, 112:144]),
        (ret_l.at[:, 112:144], rcv_r.at[:, 0:32]),
        (ret_r.at[:, 0:32], rcv_l.at[:, 112:144]),
        (ret_r.at[:, 112:144], rcv_l.at[:, 0:32]),
    )
    ret = [
        remote(src, dst, ret_ss.at[i], ret_rs.at[i], neighbour(*NEIGHBOURS[i]))
        for i, (src, dst) in enumerate(ret_parts)
    ]
    for c in ret:
        c.start()

    bias_sum = jnp.zeros((2 * HEADS, 128), F32)
    for i in range(BQ):
        sums = sg_sum[:, i, :]
        high = sums.astype(BF)
        low = (sums - high.astype(F32)).astype(BF)
        bias_sum = bias_sum + dot(jnp.concatenate([high, low], axis=0), ohv[i], NN)
    bias_sum = bias_sum[:HEADS] + bias_sum[HEADS:]
    per = HEADS // GROUP
    bias_a[...] = jnp.zeros_like(bias_a)
    for i in range(GROUP):
        bias_a[i, :per] = bias_sum[i * per : (i + 1) * per]

    def ba_copy(k):
        yy, cc, to = member(k)
        return remote(bias_a.at[yy * CORES + cc], bias_ain.at[k], ba_ss.at[k], ba_rs.at[k], to)

    @pl.loop(1, GROUP)
    def _(k):
        ba_copy(k).start()

    go_own.wait()
    at_own.wait()

    @pl.loop(1, GROUP)
    def _(k):
        go_copy(k).wait()
        at_copy(k).wait()

    wt[...] = dot(at[...], go[...].reshape(GROUP * CELLS, OUTS), NN).reshape(PIECES, PROWS, OUTS).astype(BF)

    def piece(ref, n, base_row=0, base_col=0):
        lanes = pl.ds(pl.multiple_of(base_col + n % 2 * PCOLS, PCOLS), PCOLS)
        return ref.at[base_row + n // 2, :, lanes]

    def rs_copy(k):
        n, to = on_ring(k)
        return remote(piece(wt, n), rs.at[k], rs_ss.at[k], rs_rs.at[k], to)

    @pl.loop(1, RING)
    def _(k):
        rs_copy(k).start()

    rs_own = local(piece(wt, me_ring), rs.at[0], 8)
    rs_own.start()

    @pl.loop(1, GROUP)
    def _(k):
        ba_copy(k).wait()

    bias_ain[0] = bias_a[me_group]
    bias_b[0] = jnp.sum(bias_ain[...], axis=0)

    def bx_copy(k):
        return remote(
            bias_b.at[0], bias_xin.at[k], bx_ss.at[k], bx_rs.at[k], device((x + k) % NX, y, z, core)
        )

    def bz_copy(k):
        return remote(
            bias_b.at[1], bias_zin.at[k], bz_ss.at[k], bz_rs.at[k], device(x, y, (z + k) % NZ, core)
        )

    @pl.loop(1, NX)
    def _(k):
        bx_copy(k).start()

    rs_own.wait()

    @pl.loop(1, RING)
    def _(k):
        rs_copy(k).wait()

    total = jnp.sum(rs[...].astype(F32), axis=0)
    wt_final = total.astype(BF)
    out[y * (PIECES) + me_ring // 2, :, pl.ds(pl.multiple_of(core * OUTS + me_ring % 2 * PCOLS, PCOLS), PCOLS)] = wt_final
    mine = piece(out, me_ring, y * PIECES, core * OUTS)

    def ag_copy(k):
        return remote(mine, mine, ag_ss.at[k], ag_rs.at[k], on_ring(k)[1])

    @pl.loop(1, RING)
    def _(k):
        ag_copy(k).start()

    @pl.loop(1, NX)
    def _(k):
        bx_copy(k).wait()

    bias_xin[0] = bias_b[0]
    bias_b[1] = jnp.sum(bias_xin[...], axis=0)

    @pl.loop(1, NZ)
    def _(k):
        bz_copy(k).start()

    for c in ret:
        c.wait()
    home = home_ref[...]
    for i, ref in enumerate((gk_ref, gv_ref)):
        back = jnp.concatenate([rcv_l[i], rcv_r[i]], axis=0)
        total = acc_mid[i, RAD * CW : (RAD + CH) * CW] + dot(home, back, NN)
        gap = jnp.zeros((CELLS - RAD * CW, D), F32)
        above = up_in[i].astype(F32).reshape(RAD * CW, D)
        below = down_in[i].astype(F32).reshape(RAD * CW, D)
        total = total + jnp.concatenate([above, gap], axis=0) + jnp.concatenate([gap, below], axis=0)
        ref[...] = total.astype(BF)

    @pl.loop(1, RING)
    def _(k):
        ag_copy(k).wait()

    quarter = out.at[pl.ds(y * PIECES, PIECES), :, own_lanes]

    def y_copy(k):
        return remote(quarter, quarter, y_ss.at[k], y_rs.at[k], device(x, (y + k) % NY, z, core))

    @pl.loop(1, NY)
    def _(k):
        y_copy(k).start()

    def c_copy(k):
        part = out.at[pl.ds((y + NY - k) % NY * PIECES, PIECES), :, own_lanes]
        return remote(part, part, c_ss.at[k], c_rs.at[k], device(x, y, z, 1 - core))

    c_copy(0).start()

    @pl.loop(1, NZ)
    def _(k):
        bz_copy(k).wait()

    bias_zin[0] = bias_b[1]
    bias_c[me_group] = jnp.sum(bias_zin[...], axis=0)
    bias_mine = bias_c.at[me_group]

    def bd_copy(k):
        return remote(bias_mine, bias_mine, bd_ss.at[k], bd_rs.at[k], member(k)[2])

    @pl.loop(1, GROUP)
    def _(k):
        bd_copy(k).start()

    @pl.loop(1, NY)
    def _(k):
        y_copy(k).wait()
        c_copy(k).start()

    @pl.loop(1, GROUP)
    def _(k):
        bd_copy(k).wait()

    ob_ref[...] = jnp.concatenate([bias_c[i, :per, : KS * KS] for i in range(GROUP)], axis=0)

    @pl.loop(0, NY)
    def _(k):
        c_copy(k).wait()

    store = local(out, ow_hbm, 9)
    store.start()
    store.wait()


def on_device(queries, keys, values, grad_out, out_weight, rel_bias):
    one_hot, places, pack, spread, home, heads = tables()
    cells_out = jax.ShapeDtypeStruct((CELLS, D), BF)
    dma = pltpu.SemaphoreType.DMA
    vm = pltpu.VMEM
    in_hbm = pl.BlockSpec(memory_space=pl.ANY)
    in_vmem = pl.BlockSpec(memory_space=pltpu.VMEM)
    scratch = [
        vm((CH, CW, D), BF),
        vm((CH, CW, D), BF),
        vm((D, D), BF),
        vm((BQ, KEYS, 128), BF),
        vm((2, EXT, CW, D), BF),
        vm((2, 80, D), BF),
        vm((2, 80, D), BF),
        vm((2, STAGE, D), BF),
        vm((2, STAGE, D), BF),
        vm((CELLS, D), BF),
        vm((BLOCKS, KEYS, D), BF),
        vm((BLOCKS, KEYS, D), BF),
        vm((HEADS, BQ, KEYS), F32),
        vm((16, 4 * BQ, KEYS), F32),
        vm((CELLS, D), BF),
        vm((D, CELLS), BF),
        vm((FEATS, GROUP * CELLS), BF),
        vm((GROUP, CH, CW, OUTS), BF),
        vm((HEADS, BQ, KEYS), F32),
        vm((2, EXT * CW, D), F32),
        vm((2, STAGE, D), F32),
        vm((2, STAGE, D), F32),
        vm((2, STAGE, D), BF),
        vm((2, STAGE, D), BF),
        vm((2, STAGE, D), BF),
        vm((2, STAGE, D), BF),
        vm((2, RAD, CW, D), BF),
        vm((2, RAD, CW, D), BF),
        vm((2, RAD, CW, D), BF),
        vm((2, RAD, CW, D), BF),
        vm((PIECES, PROWS, OUTS), BF),
        vm((RING, PROWS, PCOLS), BF),
        vm((D // PROWS, PROWS, D), BF),
        vm((GROUP, 8, 128), F32),
        vm((GROUP, 8, 128), F32),
        vm((NX, 8, 128), F32),
        vm((2, 8, 128), F32),
        vm((NZ, 8, 128), F32),
        vm((GROUP, 8, 128), F32),
        vm((GROUP, 8, 128), F32),
        dma((10,)),
    ]
    for count in (8, GROUP, GROUP, 8, RING, RING, NY, NY, GROUP, NX, NZ, GROUP):
        scratch += [dma((count,)), dma((count,))]
    results = pl.pallas_call(
        kernel,
        out_shape=(
            cells_out,
            cells_out,
            cells_out,
            jax.ShapeDtypeStruct((D // PROWS, PROWS, D), BF),
            jax.ShapeDtypeStruct((HEADS, KS * KS), F32),
        ),
        in_specs=[in_hbm] * 5 + [in_vmem, in_hbm] + [in_vmem] * 5,
        out_specs=(in_vmem, in_vmem, in_vmem, in_hbm, in_vmem),
        scratch_shapes=scratch,
        compiler_params=pltpu.CompilerParams(
            collective_id=0, has_side_effects=True, vmem_limit_bytes=56 * 2**20
        ),
        cost_estimate=pl.CostEstimate(flops=3 * 10**9, bytes_accessed=8 * 2**20, transcendentals=10**6),
        name="attention_backward",
    )(queries, keys, values, grad_out, out_weight, rel_bias, one_hot, places, pack, spread, home, heads)
    gq, gk, gv, gw, gb = results
    shape = queries.shape
    return gq.reshape(shape), gk.reshape(shape), gv.reshape(shape), gw.reshape(D, D), gb


def solution(mesh):
    cells = P("row", "col", None)
    return jax.shard_map(
        on_device,
        mesh=mesh,
        in_specs=(cells, cells, cells, cells, P(), P()),
        out_specs=(cells, cells, cells, P(), P()),
        check_vma=False,
    )
```

time: 486 us -> 105 us (0.22)
  the two profiles are of different devices: /device:TPU:7 before, /device:TPU:1 now
where the time goes in v1:
time: 105 us; the launch traced here: 104 us
  Pallas kernels  95.1 us (91%)
  local copies, waits for them, and re-layouts  8.7 us (8%)
    pallas_call x1, Pallas kernels, on_device(): pl.pallas_call(kernel, out_shape=(cells_out, cells_out, cells_out, jax.Sh...  95.1 us
    unnamed x7, local copies, waits for them, and re-layouts  8.7 us

profile of v1, /device:TPU:1, one launch (start us, length us, event | category | flops | bytes accessed | tf_op | source)
XLA Modules:
  0.0 104.4 jit_solution(12859639667107540849)
XLA Ops:
  0.6 95.1 %attention_backward.1 = (bf16[128,1024]{1,0:T(8,128)(2,1)}, bf16[128,1024]{1,0:T(8,128)(2,1)}, bf16[128,1024]{1,0:T(8,128)(2,1)}, bf16[64,16,1024]{2,1,0:T(8,128)(2,1)}, f32[16,121]{1,0:T(8,128)}) custom-call(bf16[16,8,1024]{2,1,0:T(8,128)(2,1)} %q_hbm.1, bf16[16,8,1024]{2,1,0:T(8,128)(2,1)} %k_hbm.1, bf16[16,8,1024]{2,1,0:T(8,128)(2,1)} %v_hbm.1, ...), custom_call_target="tpu_custom_call" | custom-call | flops 3000000000 | bytes 8388608 | tf_op jit(solution)/shard_map/attention_backward/pallas_call | solution.py:523
  95.7 1.7 %copy.22 = bf16[16,8,1024]{2,1,0:T(8,128)(2,1)} copy(bf16[16,8,1024]{2,1,0:T(8,128)(2,1)} %bitcast.7) | data formatting | bytes 524288
  97.4 1.7 %copy.23 = bf16[16,8,1024]{2,1,0:T(8,128)(2,1)} copy(bf16[16,8,1024]{2,1,0:T(8,128)(2,1)} %bitcast.6) | data formatting | bytes 524288
  99.0 1.7 %copy.24 = bf16[16,8,1024]{2,1,0:T(8,128)(2,1)} copy(bf16[16,8,1024]{2,1,0:T(8,128)(2,1)} %bitcast.5) | data formatting | bytes 524288
  100.7 0.0 copy-start
  100.7 3.1 %copy.25 = bf16[1024,1024]{1,0:T(8,128)(2,1)} copy(bf16[1024,1024]{1,0:T(8,128)(2,1)} %bitcast.4) | data formatting | bytes 4194304
  103.8 0.0 copy-done
  103.8 0.6 copy.26
Async XLA Ops:
  100.7 3.1 %copy-start = (f32[16,121]{1,0:T(8,128)S(1)}, f32[16,121]{1,0:T(8,128)}, u32[]{:S(2)}) copy-start(f32[16,121]{1,0:T(8,128)} %get-tuple-element.24) | copy-start | bytes 23236

commit v2 on v1

v2 whole, which is shorter than its diff:
```python
import functools
import math

import jax
import jax.numpy as jnp
import numpy as np
from jax import lax
from jax.experimental import pallas as pl
from jax.experimental.pallas import tpu as pltpu
from jax.sharding import PartitionSpec as P

MESH = pl.DeviceIdType.MESH
BF = jnp.bfloat16
F32 = jnp.float32

RAD = 5
KS = 11
D = 1024
HEADS = 16
CH = 16
CW = 8
CELLS = CH * CW
XLO, NY, NZ, XHI, CORES = 2, 4, 8, 2, 2
NX = XLO * XHI
GROUP = NY * CORES
BLOCKS = 4
BROWS = CH // BLOCKS
BQ = BROWS * CW
MIDK = (BROWS + 2 * RAD) * CW
SIDEK = 72
KEYS = MIDK + 2 * SIDEK
STAGE = 144
EXT = CH + 2 * RAD
FEATS = D // NY
OUTS = D // CORES
PROWS = 16
XPIECES = FEATS // PROWS // NX
NEG = -1e30
NEIGHBOURS = ((0, -1), (0, 1), (-1, 0), (1, 0), (-1, -1), (1, -1), (-1, 1), (1, 1))


def key_places():
    rows = np.full(KEYS, 1000, np.int64)
    cols = np.full(KEYS, 1000, np.int64)
    mid = np.arange(MIDK)
    rows[:MIDK], cols[:MIDK] = mid // CW, mid % CW
    side = np.arange(70)
    for first, base in ((MIDK, -RAD), (MIDK + SIDEK, CW)):
        rows[first + 1 : first + 71] = side // RAD
        cols[first + 1 : first + 71] = base + side % RAD
    return rows, cols


def tables():
    rows, cols = key_places()
    query = np.arange(BQ)
    dr = rows[None, :] - RAD - (query // CW)[:, None]
    dc = cols[None, :] - (query % CW)[:, None]
    inside = (np.abs(dr) <= RAD) & (np.abs(dc) <= RAD)
    offsets = np.where(inside, (dr + RAD) * KS + dc + RAD, 127)
    one_hot = offsets[:, :, None] == np.arange(128)[None, None, :]
    places = np.zeros((8, KEYS), np.int32)
    places[0], places[1] = rows, cols
    pack = np.zeros((2 * 80, CELLS), bool)
    edge = np.arange(80)
    pack[edge, edge // RAD * CW + edge % RAD] = True
    pack[80 + edge, edge // RAD * CW + CW - RAD + edge % RAD] = True
    spread = np.zeros((BLOCKS * SIDEK, STAGE), bool)
    for b in range(BLOCKS):
        place = np.arange(SIDEK)
        spread[b * SIDEK + place, 6 + 20 * b + place] = True
    join = np.zeros((2 * STAGE, BLOCKS * 2 * SIDEK), bool)
    for b in range(BLOCKS):
        place = np.arange(SIDEK)
        join[6 + 20 * b + place, 2 * SIDEK * b + place] = True
        join[STAGE + 6 + 20 * b + place, 2 * SIDEK * b + SIDEK + place] = True
    entry = np.arange(STAGE)
    cell = np.where(entry < 32, entry, np.where(entry < 112, entry - 32, entry - 64))
    home = np.zeros((CELLS, 2 * STAGE), bool)
    home[cell // RAD * CW + cell % RAD, entry] = True
    home[cell // RAD * CW + CW - RAD + cell % RAD, STAGE + entry] = True
    heads = np.repeat(np.arange(4), BQ)[:, None] == (np.arange(256) // 64)[None, :]
    as_low = lambda t: np.asarray(t, np.float32).astype(jnp.bfloat16)
    return (as_low(one_hot), places, as_low(pack), as_low(spread), as_low(join), as_low(home), as_low(heads))


def dot(a, b, dims):
    return lax.dot_general(a, b, ((dims[0], dims[1]), ((), ())), preferred_element_type=F32)


NN = ((1,), (0,))
NT = ((1,), (1,))
TN = ((0,), (0,))


def kernel(
    q_hbm, k_hbm, v_hbm, g_hbm, w_hbm, bias_ref, oh_hbm, places_ref, pack_ref, spread_ref, join_ref, home_ref, heads_ref,
    gq_hbm, gk_hbm, gv_hbm, ow_hbm, ob_ref,
    qv, gv, wv, ohv, mid, panel_l, panel_r, stage_l, stage_r, ga, kb, vb, table, probs, att, at, go,
    sg_sum, acc_mid, side, ret_l, ret_r, rcv_l, rcv_r, up_out, down_out, up_in, down_in,
    gq, gk, gval, wt, rx, wz, rz, out, bias_a, bias_ain, bias_xin, bias_b, bias_zin, bias_c,
    loc_sem, halo_ss, halo_rs, go_ss, go_rs, at_ss, at_rs, ret_ss, ret_rs, rx_ss, rx_rs, rz_ss, rz_rs, zg_ss, zg_rs,
    a2_ss, a2_rs, b2_ss, b2_rs, a3_ss, a3_rs, b3_ss, b3_rs, ca_ss, ca_rs, cb_ss, cb_rs,
    ba_ss, ba_rs, bx_ss, bx_rs, bz_ss, bz_rs, bd_ss, bd_rs,
):
    row, col = lax.axis_index("row"), lax.axis_index("col")
    nrow, ncol = XLO * NY, NZ * XHI * CORES
    x = (col // CORES) % XHI * XLO + row // NY
    y, z, core = row % NY, col // (XHI * CORES), col % CORES
    scale = 1.0 / math.sqrt(D // HEADS)

    def device(x_at, y_at, z_at, core_at):
        return (x_at % XLO * NY + y_at, (z_at * XHI + x_at // XLO) * CORES + core_at)

    def neighbour(dr, dc):
        return ((row + dr + nrow) % nrow, (col + dc + ncol) % ncol)

    def member(k):
        yy = (y + k // CORES) % NY
        cc = (core + k % CORES) % CORES
        return yy, cc, device(x, yy, z, cc)

    def along_x(k):
        return device((x + k) % NX, y, z, core)

    def along_y(k):
        return device(x, (y + k) % NY, z, core)

    def along_z(k):
        return device(x, y, (z + k) % NZ, core)

    me_group = y * CORES + core

    def local(src, dst, at_sem):
        return pltpu.make_async_copy(src, dst, loc_sem.at[at_sem])

    def remote(src, dst, ss, rsem, to):
        return pltpu.make_async_remote_copy(
            src_ref=src, dst_ref=dst, send_sem=ss, recv_sem=rsem, device_id=to, device_id_type=MESH
        )

    loads = [
        local(k_hbm, mid.at[0, RAD : RAD + CH], 0),
        local(v_hbm, mid.at[1, RAD : RAD + CH], 1),
        local(g_hbm, gv, 2),
        local(w_hbm, wv, 3),
        local(q_hbm, qv, 4),
        local(oh_hbm, ohv, 5),
    ]
    for c in loads:
        c.start()
    barrier = pltpu.get_barrier_semaphore()
    for dr, dc in NEIGHBOURS:
        pl.semaphore_signal(barrier, inc=1, device_id=neighbour(dr, dc), device_id_type=MESH)

    @pl.loop(1, GROUP)
    def _(k):
        pl.semaphore_signal(barrier, inc=1, device_id=member(k)[2], device_id_type=MESH)

    @pl.loop(1, NX)
    def _(k):
        pl.semaphore_signal(barrier, inc=1, device_id=along_x(k), device_id_type=MESH)

    @pl.loop(1, NZ)
    def _(k):
        pl.semaphore_signal(barrier, inc=1, device_id=along_z(k), device_id_type=MESH)

    loads[0].wait()
    loads[1].wait()
    for i in range(2):
        own = mid[i, RAD : RAD + CH].reshape(CELLS, D)
        packed = dot(pack_ref[...], own, NN).astype(BF)
        panel_l[i] = packed[:80]
        panel_r[i] = packed[80:]
    pl.semaphore_wait(barrier, len(NEIGHBOURS) + GROUP - 1 + NX - 1 + NZ - 1)

    halo_parts = (
        (panel_l, stage_r.at[:, 32:112]),
        (panel_r, stage_l.at[:, 32:112]),
        (mid.at[:, RAD : 2 * RAD], mid.at[:, RAD + CH :]),
        (mid.at[:, CH : CH + RAD], mid.at[:, :RAD]),
        (panel_l.at[:, 0:32], stage_r.at[:, 112:144]),
        (panel_l.at[:, 48:80], stage_r.at[:, 0:32]),
        (panel_r.at[:, 0:32], stage_l.at[:, 112:144]),
        (panel_r.at[:, 48:80], stage_l.at[:, 0:32]),
    )
    halo = [
        remote(src, dst, halo_ss.at[i], halo_rs.at[i], neighbour(*NEIGHBOURS[i]))
        for i, (src, dst) in enumerate(halo_parts)
    ]
    for c in halo:
        c.start()

    loads[2].wait()

    def go_copy(k):
        yy, cc, to = member(k)
        lanes = pl.ds(pl.multiple_of(cc * OUTS, OUTS), OUTS)
        return remote(gv.at[:, :, lanes], go.at[me_group], go_ss.at[k], go_rs.at[k], to)

    @pl.loop(1, GROUP)
    def _(k):
        go_copy(k).start()

    own_lanes = pl.ds(pl.multiple_of(core * OUTS, OUTS), OUTS)
    go_own = local(gv.at[:, :, own_lanes], go.at[me_group], 6)
    go_own.start()

    loads[3].wait()
    ga[...] = dot(gv[...].reshape(CELLS, D), wv[...], NT).astype(BF)

    loads[5].wait()
    padded = jnp.concatenate([bias_ref[...], jnp.full((HEADS, 128 - KS * KS), NEG, F32)], axis=1)
    high = padded.astype(BF)
    rest = padded - high.astype(F32)
    middle = rest.astype(BF)
    low = (rest - middle.astype(F32)).astype(BF)
    three = jnp.concatenate([high, middle, low], axis=0)
    for i in range(BQ):
        terms = dot(three, ohv[i], NT)
        table[:, i, :] = terms[:HEADS] + terms[HEADS : 2 * HEADS] + terms[2 * HEADS :]
    for ref in (acc_mid, sg_sum):
        ref[...] = jnp.zeros_like(ref)

    loads[4].wait()
    halo[2].wait()
    halo[3].wait()
    for i, slab in enumerate((kb, vb)):
        for b in range(BLOCKS):
            slab[b, :MIDK] = mid[i, b * BROWS : b * BROWS + BROWS + 2 * RAD].reshape(MIDK, D)
    for i in (0, 1, 4, 5, 6, 7):
        halo[i].wait()
    for i, slab in enumerate((kb, vb)):
        left = dot(spread_ref[...], stage_l[i], NN)
        right = dot(spread_ref[...], stage_r[i], NN)
        for b in range(BLOCKS):
            rows = slice(b * SIDEK, (b + 1) * SIDEK)
            slab[b, MIDK:] = jnp.concatenate([left[rows], right[rows]], axis=0).astype(BF)

    mask_low = heads_ref[...]
    mask_wide = mask_low.astype(F32)

    def spread_heads(tile):
        return jnp.concatenate([tile] * 4, axis=0) * mask_low

    def fold_heads(full):
        return jnp.sum((full * mask_wide).reshape(4, BQ, 256), axis=0)

    key_row, key_col = places_ref[0:1, :], places_ref[1:2, :]
    grid_col = col * CW + key_col
    col_ok = (grid_col >= 0) & (grid_col < ncol * CW)
    q2 = qv[...].reshape(CELLS, D)
    groups = [slice(h * 256, (h + 1) * 256) for h in range(4)]

    def forward(b):
        cells = slice(b * BQ, (b + 1) * BQ)
        grid_row = row * CH + b * BROWS - RAD + key_row
        present = col_ok & (grid_row >= 0) & (grid_row < nrow * CH)
        absent = jnp.where(present, 0.0, NEG)
        scores = [dot(spread_heads(q2[cells, n]), kb[b, :, n], NT) for n in groups]
        scores = [
            s * scale + (table[4 * h : 4 * h + 4].reshape(4 * BQ, KEYS) + absent) for h, s in enumerate(scores)
        ]
        weights = [jnp.exp(s - jnp.max(s, axis=1, keepdims=True)) for s in scores]
        p = [e * (1.0 / jnp.sum(e, axis=1, keepdims=True)) for e in weights]
        for h in range(4):
            probs[b * 4 + h] = p[h]
        full = [dot(t.astype(BF), vb[b, :, n], NN) for t, n in zip(p, groups)]
        for t, n in zip(full, groups):
            att[cells, n] = fold_heads(t).astype(BF)

    half_cells = CELLS // 2

    def at_copy(part, k):
        yy, cc, to = member(k)
        src = att.at[pl.ds(part * half_cells, half_cells), pl.ds(pl.multiple_of(yy * FEATS, FEATS), FEATS)]
        dst = at.at[me_group, pl.ds(part * half_cells, half_cells)]
        return remote(src, dst, at_ss.at[part, k], at_rs.at[part, k], to)

    for part in range(2):
        forward(2 * part)
        forward(2 * part + 1)

        @pl.loop(1, GROUP)
        def _(k):
            at_copy(part, k).start()

    at_own = local(att.at[:, pl.ds(pl.multiple_of(y * FEATS, FEATS), FEATS)], at.at[me_group], 7)
    at_own.start()

    def backward(b):
        cells = slice(b * BQ, (b + 1) * BQ)
        qm = [spread_heads(q2[cells, n]) for n in groups]
        gm = [spread_heads(ga[cells, n]) for n in groups]
        p = [probs[b * 4 + h] for h in range(4)]
        dp = [dot(g, vb[b, :, n], NT) for g, n in zip(gm, groups)]
        sg = [t * (d - jnp.sum(t * d, axis=1, keepdims=True)) for t, d in zip(p, dp)]
        for h in range(4):
            sg_sum[4 * h : 4 * h + 4] += sg[h].reshape(4, BQ, KEYS)
        sl = [t.astype(BF) for t in sg]
        for h, n in enumerate(groups):
            gq[cells, n] = (fold_heads(dot(sl[h], kb[b, :, n], NN)) * scale).astype(BF)
            parts = (dot(sl[h], qm[h], TN) * scale, dot(p[h].astype(BF), gm[h], TN))
            for i, part in enumerate(parts):
                acc_mid[i, b * BQ : b * BQ + MIDK, n] += part[:MIDK]
                side[i, b * 2 * SIDEK : (b + 1) * 2 * SIDEK, n] = part[MIDK:].astype(BF)

    backward(0)
    backward(1)
    go_own.wait()
    at_own.wait()

    @pl.loop(1, GROUP)
    def _(k):
        go_copy(k).wait()
        at_copy(0, k).wait()
        at_copy(1, k).wait()

    wt[...] = dot(at[...].reshape(GROUP * CELLS, FEATS), go[...].reshape(GROUP * CELLS, OUTS), TN).reshape(FEATS // PROWS, PROWS, OUTS).astype(BF)

    def rx_copy(k):
        part = wt.at[pl.ds((x + k) % NX * XPIECES, XPIECES)]
        return remote(part, rx.at[k], rx_ss.at[k], rx_rs.at[k], along_x(k))

    @pl.loop(1, NX)
    def _(k):
        rx_copy(k).start()

    rx_own = local(wt.at[pl.ds(x * XPIECES, XPIECES)], rx.at[0], 8)
    rx_own.start()
    backward(2)
    backward(3)
    gq_store = local(gq, gq_hbm, 9)
    gq_store.start()

    for i in range(2):
        joined = dot(join_ref[...], side[i], NN).astype(BF)
        ret_l[i] = joined[:STAGE]
        ret_r[i] = joined[STAGE:]
    up_out[...] = acc_mid[:, : RAD * CW].reshape(2, RAD, CW, D).astype(BF)
    down_out[...] = acc_mid[:, (RAD + CH) * CW :].reshape(2, RAD, CW, D).astype(BF)
    ret_parts = (
        (ret_l.at[:, 32:112], rcv_r.at[:, 32:112]),
        (ret_r.at[:, 32:112], rcv_l.at[:, 32:112]),
        (up_out, down_in),
        (down_out, up_in),
        (ret_l.at[:, 0:32], rcv_r.at[:, 112:144]),
        (ret_l.at[:, 112:144], rcv_r.at[:, 0:32]),
        (ret_r.at[:, 0:32], rcv_l.at[:, 112:144]),
        (ret_r.at[:, 112:144], rcv_l.at[:, 0:32]),
    )
    ret = [
        remote(src, dst, ret_ss.at[i], ret_rs.at[i], neighbour(*NEIGHBOURS[i]))
        for i, (src, dst) in enumerate(ret_parts)
    ]
    for c in ret:
        c.start()

    rx_own.wait()

    @pl.loop(1, NX)
    def _(k):
        rx_copy(k).wait()

    total = jnp.sum(rx[...].astype(F32), axis=0).astype(BF)
    half = OUTS // 2
    for i in range(XPIECES):
        for j in range(2):
            first, second = total[i, :, j * 128 : j * 128 + 128], total[i, :, half + j * 128 : half + j * 128 + 128]
            wz[2 * i + j] = jnp.concatenate([first, second], axis=1)

    def rz_copy(k):
        return remote(wz.at[(z + k) % NZ], rz.at[k], rz_ss.at[k], rz_rs.at[k], along_z(k))

    @pl.loop(1, NZ)
    def _(k):
        rz_copy(k).start()

    bias_sum = jnp.zeros((2 * HEADS, 128), F32)
    for i in range(BQ):
        sums = sg_sum[:, i, :]
        high = sums.astype(BF)
        low = (sums - high.astype(F32)).astype(BF)
        bias_sum = bias_sum + dot(jnp.concatenate([high, low], axis=0), ohv[i], NN)
    bias_sum = bias_sum[:HEADS] + bias_sum[HEADS:]
    per = HEADS // GROUP
    bias_a[...] = jnp.zeros_like(bias_a)
    for i in range(GROUP):
        bias_a[i, :per] = bias_sum[i * per : (i + 1) * per]

    def ba_copy(k):
        yy, cc, to = member(k)
        return remote(bias_a.at[yy * CORES + cc], bias_ain.at[k], ba_ss.at[k], ba_rs.at[k], to)

    @pl.loop(1, GROUP)
    def _(k):
        ba_copy(k).start()

    rz[0] = wz[z]

    @pl.loop(1, NZ)
    def _(k):
        rz_copy(k).wait()

    final = jnp.sum(rz[...].astype(F32), axis=0).astype(BF)
    spot = x * XPIECES + z // 2
    out[core, 0, y, spot, z % 2] = final[:, :128]
    out[core, 1, y, spot, z % 2] = final[:, 128:]
    mine = out.at[core, :, y, spot, z % 2]

    def zg_copy(k):
        return remote(mine, mine, zg_ss.at[k], zg_rs.at[k], along_z(k))

    @pl.loop(1, NZ)
    def _(k):
        zg_copy(k).start()

    @pl.loop(1, GROUP)
    def _(k):
        ba_copy(k).wait()

    bias_ain[0] = bias_a[me_group]
    bias_b[0] = jnp.sum(bias_ain[...], axis=0)

    def bx_copy(k):
        return remote(bias_b.at[0], bias_xin.at[k], bx_ss.at[k], bx_rs.at[k], along_x(k))

    def bz_copy(k):
        return remote(bias_b.at[1], bias_zin.at[k], bz_ss.at[k], bz_rs.at[k], along_z(k))

    @pl.loop(1, NX)
    def _(k):
        bx_copy(k).start()

    @pl.loop(1, NZ)
    def _(k):
        zg_copy(k).wait()

    slab_a = out.at[core, 0, y, pl.ds(x * XPIECES, XPIECES)]
    slab_b = out.at[core, 1, y, pl.ds(x * XPIECES, XPIECES)]

    def a2_copy(k):
        return remote(slab_a, slab_a, a2_ss.at[k], a2_rs.at[k], along_x(k))

    def b2_copy(k):
        return remote(slab_b, slab_b, b2_ss.at[k], b2_rs.at[k], along_y(k))

    @pl.loop(1, NX)
    def _(k):
        a2_copy(k).start()

    @pl.loop(1, NY)
    def _(k):
        b2_copy(k).start()

    @pl.loop(1, NX)
    def _(k):
        bx_copy(k).wait()

    bias_xin[0] = bias_b[0]
    bias_b[1] = jnp.sum(bias_xin[...], axis=0)

    @pl.loop(1, NZ)
    def _(k):
        bz_copy(k).start()

    def part_a(k):
        return out.at[core, 0, (y + k + NY) % NY]

    def part_b(k):
        return out.at[core, 1, :, pl.ds((x + k + NX) % NX * XPIECES, XPIECES)]

    def a3_copy(k):
        return remote(part_a(0), part_a(0), a3_ss.at[k], a3_rs.at[k], along_y(k))

    def b3_copy(k):
        return remote(part_b(0), part_b(0), b3_ss.at[k], b3_rs.at[k], along_x(k))

    def ca_copy(k):
        return remote(part_a(-k), part_a(-k), ca_ss.at[k], ca_rs.at[k], device(x, y, z, 1 - core))

    def cb_copy(k):
        return remote(part_b(-k), part_b(-k), cb_ss.at[k], cb_rs.at[k], device(x, y, z, 1 - core))

    @pl.loop(1, NX)
    def _(k):
        a2_copy(k).wait()

    @pl.loop(1, NY)
    def _(k):
        a3_copy(k).start()

    @pl.loop(1, NY)
    def _(k):
        b2_copy(k).wait()

    @pl.loop(1, NX)
    def _(k):
        b3_copy(k).start()

    ca_copy(0).start()
    cb_copy(0).start()

    for c in ret:
        c.wait()
    home = home_ref[...]
    grad_stores = []
    for i, (ref, hbm) in enumerate(((gk, gk_hbm), (gval, gv_hbm))):
        back = jnp.concatenate([rcv_l[i], rcv_r[i]], axis=0)
        total = acc_mid[i, RAD * CW : (RAD + CH) * CW] + dot(home, back, NN)
        gap = jnp.zeros((CELLS - RAD * CW, D), F32)
        above = up_in[i].astype(F32).reshape(RAD * CW, D)
        below = down_in[i].astype(F32).reshape(RAD * CW, D)
        total = total + jnp.concatenate([above, gap], axis=0) + jnp.concatenate([gap, below], axis=0)
        ref[...] = total.astype(BF)
        grad_stores.append(local(ref, hbm, 10 + i))
        grad_stores[-1].start()

    @pl.loop(1, NZ)
    def _(k):
        bz_copy(k).wait()

    bias_zin[0] = bias_b[1]
    bias_c[me_group] = jnp.sum(bias_zin[...], axis=0)
    bias_mine = bias_c.at[me_group]

    def bd_copy(k):
        return remote(bias_mine, bias_mine, bd_ss.at[k], bd_rs.at[k], member(k)[2])

    @pl.loop(1, GROUP)
    def _(k):
        bd_copy(k).start()

    @pl.loop(1, NY)
    def _(k):
        a3_copy(k).wait()
        ca_copy(k).start()
        b3_copy(k).wait()
        cb_copy(k).start()

    def stores(of_core, first):
        made = []
        for i in range(2):
            for j in range(2):
                lanes = pl.ds(pl.multiple_of(of_core * OUTS + i * half + j * 128, 128), 128)
                made.append(local(out.at[of_core, i, :, :, j], ow_hbm.at[:, :, :, lanes], first + 2 * i + j))
        return made

    kept = stores(core, 12)
    for c in kept:
        c.start()

    @pl.loop(1, GROUP)
    def _(k):
        bd_copy(k).wait()

    ob_ref[...] = jnp.concatenate([bias_c[i, :per, : KS * KS] for i in range(GROUP)], axis=0)

    @pl.loop(0, NY)
    def _(k):
        ca_copy(k).wait()
        cb_copy(k).wait()

    given = stores(1 - core, 16)
    for c in given:
        c.start()
    for c in (gq_store, *grad_stores, *kept, *given):
        c.wait()


def hand_over(*refs):
    sources, targets, held, sems = refs[:5], refs[5:10], refs[10:15], refs[15]
    pairs = []
    for i in range(5):
        chunks = range(NY) if i == 3 else (None,)
        for c in chunks:
            src, via, dst = (r if c is None else r.at[c] for r in (sources[i], held[i], targets[i]))
            at_sem = len(pairs)
            pairs.append(
                (pltpu.make_async_copy(src, via, sems.at[0, at_sem]), pltpu.make_async_copy(via, dst, sems.at[1, at_sem]))
            )
    for fetch, _ in pairs:
        fetch.start()
    for fetch, store in pairs:
        fetch.wait()
        store.start()
    for _, store in pairs:
        store.wait()


def on_device(queries, keys, values, grad_out, out_weight, rel_bias):
    one_hot, places, pack, spread, join, home, heads = tables()
    cells_out = jax.ShapeDtypeStruct((CELLS, D), BF)
    dma = pltpu.SemaphoreType.DMA
    vm = pltpu.VMEM
    in_hbm = pl.BlockSpec(memory_space=pl.ANY)
    in_vmem = pl.BlockSpec(memory_space=pltpu.VMEM)
    scratch = [
        vm((CH, CW, D), BF),
        vm((CH, CW, D), BF),
        vm((D, D), BF),
        vm((BQ, KEYS, 128), BF),
        vm((2, EXT, CW, D), BF),
        vm((2, 80, D), BF),
        vm((2, 80, D), BF),
        vm((2, STAGE, D), BF),
        vm((2, STAGE, D), BF),
        vm((CELLS, D), BF),
        vm((BLOCKS, KEYS, D), BF),
        vm((BLOCKS, KEYS, D), BF),
        vm((HEADS, BQ, KEYS), F32),
        vm((16, 4 * BQ, KEYS), F32),
        vm((CELLS, D), BF),
        vm((GROUP, CELLS, FEATS), BF),
        vm((GROUP, CH, CW, OUTS), BF),
        vm((HEADS, BQ, KEYS), F32),
        vm((2, EXT * CW, D), F32),
        vm((2, BLOCKS * 2 * SIDEK, D), BF),
        vm((2, STAGE, D), BF),
        vm((2, STAGE, D), BF),
        vm((2, STAGE, D), BF),
        vm((2, STAGE, D), BF),
        vm((2, RAD, CW, D), BF),
        vm((2, RAD, CW, D), BF),
        vm((2, RAD, CW, D), BF),
        vm((2, RAD, CW, D), BF),
        vm((CELLS, D), BF),
        vm((CELLS, D), BF),
        vm((CELLS, D), BF),
        vm((FEATS // PROWS, PROWS, OUTS), BF),
        vm((NX, XPIECES, PROWS, OUTS), BF),
        vm((NZ, PROWS, 256), BF),
        vm((NZ, PROWS, 256), BF),
        vm((CORES, 2, NY, NX * XPIECES, 2, PROWS, 128), BF),
        vm((GROUP, 8, 128), F32),
        vm((GROUP, 8, 128), F32),
        vm((NX, 8, 128), F32),
        vm((2, 8, 128), F32),
        vm((NZ, 8, 128), F32),
        vm((GROUP, 8, 128), F32),
        dma((20,)),
    ]
    for count in (8, GROUP, (2, GROUP), 8, NX, NZ, NZ, NX, NY, NY, NX, NY, NX, GROUP, NX, NZ, GROUP):
        shape = count if isinstance(count, tuple) else (count,)
        scratch += [dma(shape), dma(shape)]
    results = pl.pallas_call(
        kernel,
        out_shape=(
            cells_out,
            cells_out,
            cells_out,
            jax.ShapeDtypeStruct((NY, FEATS // PROWS, PROWS, D), BF),
            jax.ShapeDtypeStruct((HEADS, KS * KS), F32),
        ),
        in_specs=[in_hbm] * 5 + [in_vmem, in_hbm] + [in_vmem] * 6,
        out_specs=(in_hbm, in_hbm, in_hbm, in_hbm, in_vmem),
        scratch_shapes=scratch,
        compiler_params=pltpu.CompilerParams(
            collective_id=0, has_side_effects=True, vmem_limit_bytes=56 * 2**20
        ),
        cost_estimate=pl.CostEstimate(flops=3 * 10**9, bytes_accessed=8 * 2**20, transcendentals=10**6),
        name="attention_backward",
    )(queries, keys, values, grad_out, out_weight, rel_bias, one_hot, places, pack, spread, join, home, heads)
    gq, gk, gv, gw, gb = pl.pallas_call(
        hand_over,
        out_shape=tuple(jax.ShapeDtypeStruct(r.shape, r.dtype) for r in results),
        in_specs=[in_hbm] * 5,
        out_specs=(in_hbm,) * 5,
        scratch_shapes=[vm(r.shape, r.dtype) for r in results] + [dma((2, 4 + NY))],
        name="hand_over",
    )(*results)
    shape = queries.shape
    return gq.reshape(shape), gk.reshape(shape), gv.reshape(shape), gw.reshape(D, D), gb


def solution(mesh):
    cells = P("row", "col", None)
    return jax.shard_map(
        on_device,
        mesh=mesh,
        in_specs=(cells, cells, cells, cells, P(), P()),
        out_specs=(cells, cells, cells, P(), P()),
        check_vma=False,
    )
```

time: 105 us -> 89.1 us (0.85)
  local copies, waits for them, and re-layouts: 8.7 us -> 0 us
  Pallas kernels: 95.1 us -> 88.3 us
    pallas_call x1, Pallas kernels: 95.1 us -> 85.6 us  [on_device(): pl.pallas_call(kernel, out_shape=(cells_out, cells_out, cells_out, jax.Sh...]
    unnamed x7 -> x0, local copies, waits for them, and re-layouts: 8.7 us -> none
    pallas_call x0 -> x1, Pallas kernels: none -> 2.74 us  [on_device(): pl.pallas_call(hand_over, out_shape=tuple((jax.ShapeDtypeStruct(r.shape,...]
where the time goes in v2:
time: 89.1 us; the launch traced here: 88.9 us
  Pallas kernels  88.3 us (99%)
    pallas_call x1, Pallas kernels, on_device(): pl.pallas_call(kernel, out_shape=(cells_out, cells_out, cells_out, jax.Sh...  85.6 us
    pallas_call x1, Pallas kernels, on_device(): pl.pallas_call(hand_over, out_shape=tuple((jax.ShapeDtypeStruct(r.shape,...  2.74 us

profile of v2, /device:TPU:1, one launch (start us, length us, event | category | flops | bytes accessed | tf_op | source)
XLA Modules:
  0.0 88.9 jit_solution(14326976255251348459)
XLA Ops:
  0.6 85.6 %attention_backward.1 = (bf16[128,1024]{1,0:T(8,128)(2,1)}, bf16[128,1024]{1,0:T(8,128)(2,1)}, bf16[128,1024]{1,0:T(8,128)(2,1)}, bf16[4,16,16,1024]{3,2,1,0:T(8,128)(2,1)}, f32[16,121]{1,0:T(8,128)}) custom-call(bf16[16,8,1024]{2,1,0:T(8,128)(2,1)} %q_hbm.1, bf16[16,8,1024]{2,1,0:T(8,128)(2,1)} %k_hbm.1, bf16[16,8,1024]{2,1,0:T(8,128)(2,1)} %v_hbm.1, ...), custom_call_target="tpu_custom_call" | custom-call | flops 3000000000 | bytes 8388608 | tf_op jit(solution)/shard_map/attention_backward/pallas_call | solution.py:646
  86.2 2.7 %hand_over.1 = (bf16[128,1024]{1,0:T(8,128)(2,1)}, bf16[128,1024]{1,0:T(8,128)(2,1)}, bf16[128,1024]{1,0:T(8,128)(2,1)}, bf16[4,16,16,1024]{3,2,1,0:T(8,128)(2,1)}, f32[16,121]{1,0:T(8,128)}) custom-call(bf16[128,1024]{1,0:T(8,128)(2,1)} %get-tuple-element.15.refs_0_, bf16[128,1024]{1,0:T(8,128)(2,1)} %get-tuple-element.16.refs_1_, ...), custom_call_target="tpu_custom_call" | custom-call | tf_op jit(solution)/shard_map/hand_over/pallas_call | solution.py:664

commit v3 on v2

--- a/solution.py
+++ b/solution.py
@@ -66,9 +66,15 @@
     pack[edge, edge // RAD * CW + edge % RAD] = True
     pack[80 + edge, edge // RAD * CW + CW - RAD + edge % RAD] = True
     spread = np.zeros((BLOCKS * SIDEK, STAGE), bool)
+    place = np.arange(70)
     for b in range(BLOCKS):
-        place = np.arange(SIDEK)
-        spread[b * SIDEK + place, 6 + 20 * b + place] = True
+        ext = 20 * b + place
+        at = np.where(ext < 25, 80 + ext, np.where(ext < 105, ext - 25, ext))
+        spread[b * SIDEK + 1 + place, at] = True
+    strip = np.zeros((2 * 64, 2 * RAD * CW), bool)
+    corner = np.arange(50)
+    strip[corner, corner // RAD * CW + corner % RAD] = True
+    strip[64 + corner, corner // RAD * CW + CW - RAD + corner % RAD] = True
     join = np.zeros((2 * STAGE, BLOCKS * 2 * SIDEK), bool)
     for b in range(BLOCKS):
         place = np.arange(SIDEK)
@@ -81,7 +87,7 @@
     home[cell // RAD * CW + CW - RAD + cell % RAD, STAGE + entry] = True
     heads = np.repeat(np.arange(4), BQ)[:, None] == (np.arange(256) // 64)[None, :]
     as_low = lambda t: np.asarray(t, np.float32).astype(jnp.bfloat16)
-    return (as_low(one_hot), places, as_low(pack), as_low(spread), as_low(join), as_low(home), as_low(heads))
+    return (as_low(one_hot), places, as_low(pack), as_low(strip), as_low(spread), as_low(join), as_low(home), as_low(heads))
 
 
 def dot(a, b, dims):
@@ -94,11 +100,11 @@
 
 
 def kernel(
-    q_hbm, k_hbm, v_hbm, g_hbm, w_hbm, bias_ref, oh_hbm, places_ref, pack_ref, spread_ref, join_ref, home_ref, heads_ref,
-    gq_hbm, gk_hbm, gv_hbm, ow_hbm, ob_ref,
-    qv, gv, wv, ohv, mid, panel_l, panel_r, stage_l, stage_r, ga, kb, vb, table, probs, att, at, go,
+    q_hbm, k_hbm, v_hbm, g_hbm, w_hbm, bias_ref, oh_hbm, places_ref, pack_ref, strip_ref, spread_ref, join_ref, home_ref, heads_ref,
+    gq, gk, gval, out, ob_ref,
+    qv, gv, wv, ohv, mid, panel_l, panel_r, strip_l, strip_r, stage_l, stage_r, ga, kb, vb, table, probs, att, at, go,
     sg_sum, acc_mid, side, ret_l, ret_r, rcv_l, rcv_r, up_out, down_out, up_in, down_in,
-    gq, gk, gval, wt, rx, wz, rz, out, bias_a, bias_ain, bias_xin, bias_b, bias_zin, bias_c,
+    wt, rx, wz, rz, bias_a, bias_ain, bias_xin, bias_b, bias_zin, bias_c,
     loc_sem, halo_ss, halo_rs, go_ss, go_rs, at_ss, at_rs, ret_ss, ret_rs, rx_ss, rx_rs, rz_ss, rz_rs, zg_ss, zg_rs,
     a2_ss, a2_rs, b2_ss, b2_rs, a3_ss, a3_rs, b3_ss, b3_rs, ca_ss, ca_rs, cb_ss, cb_rs,
     ba_ss, ba_rs, bx_ss, bx_rs, bz_ss, bz_rs, bd_ss, bd_rs,
@@ -175,20 +181,18 @@
     pl.semaphore_wait(barrier, len(NEIGHBOURS) + GROUP - 1 + NX - 1 + NZ - 1)
 
     halo_parts = (
-        (panel_l, stage_r.at[:, 32:112]),
-        (panel_r, stage_l.at[:, 32:112]),
-        (mid.at[:, RAD : 2 * RAD], mid.at[:, RAD + CH :]),
-        (mid.at[:, CH : CH + RAD], mid.at[:, :RAD]),
-        (panel_l.at[:, 0:32], stage_r.at[:, 112:144]),
-        (panel_l.at[:, 48:80], stage_r.at[:, 0:32]),
-        (panel_r.at[:, 0:32], stage_l.at[:, 112:144]),
-        (panel_r.at[:, 48:80], stage_l.at[:, 0:32]),
+        (mid.at[:, RAD : 2 * RAD], mid.at[:, RAD + CH :], 2),
+        (mid.at[:, CH : CH + RAD], mid.at[:, :RAD], 3),
+        (panel_l, stage_r.at[:, :80], 0),
+        (panel_r, stage_l.at[:, :80], 1),
+        (strip_l, stage_r.at[:, 80:], 0),
+        (strip_r, stage_l.at[:, 80:], 1),
     )
     halo = [
-        remote(src, dst, halo_ss.at[i], halo_rs.at[i], neighbour(*NEIGHBOURS[i]))
-        for i, (src, dst) in enumerate(halo_parts)
+        remote(src, dst, halo_ss.at[i], halo_rs.at[i], neighbour(*NEIGHBOURS[n]))
+        for i, (src, dst, n) in enumerate(halo_parts)
     ]
-    for c in halo:
+    for c in halo[:4]:
         c.start()
 
     loads[2].wait()
@@ -208,6 +212,16 @@
 
     loads[3].wait()
     ga[...] = dot(gv[...].reshape(CELLS, D), wv[...], NT).astype(BF)
+
+    halo[0].wait()
+    halo[1].wait()
+    for i in range(2):
+        rims = jnp.concatenate([mid[i, :RAD], mid[i, RAD + CH :]], axis=0).reshape(2 * RAD * CW, D)
+        packed = dot(strip_ref[...], rims, NN).astype(BF)
+        strip_l[i] = packed[:64]
+        strip_r[i] = packed[64:]
+    halo[4].start()
+    halo[5].start()
 
     loads[5].wait()
     padded = jnp.concatenate([bias_ref[...], jnp.full((HEADS, 128 - KS * KS), NEG, F32)], axis=1)
@@ -222,14 +236,12 @@
     for ref in (acc_mid, sg_sum):
         ref[...] = jnp.zeros_like(ref)
 
-    loads[4].wait()
-    halo[2].wait()
-    halo[3].wait()
     for i, slab in enumerate((kb, vb)):
         for b in range(BLOCKS):
             slab[b, :MIDK] = mid[i, b * BROWS : b * BROWS + BROWS + 2 * RAD].reshape(MIDK, D)
-    for i in (0, 1, 4, 5, 6, 7):
-        halo[i].wait()
+    loads[4].wait()
+    for c in halo[2:]:
+        c.wait()
     for i, slab in enumerate((kb, vb)):
         left = dot(spread_ref[...], stage_l[i], NN)
         right = dot(spread_ref[...], stage_r[i], NN)
@@ -330,8 +342,6 @@
     rx_own.start()
     backward(2)
     backward(3)
-    gq_store = local(gq, gq_hbm, 9)
-    gq_store.start()
 
     for i in range(2):
         joined = dot(join_ref[...], side[i], NN).astype(BF)
@@ -353,8 +363,6 @@
         remote(src, dst, ret_ss.at[i], ret_rs.at[i], neighbour(*NEIGHBOURS[i]))
         for i, (src, dst) in enumerate(ret_parts)
     ]
-    for c in ret:
-        c.start()
 
     rx_own.wait()
 
@@ -375,6 +383,9 @@
     @pl.loop(1, NZ)
     def _(k):
         rz_copy(k).start()
+
+    for c in ret:
+        c.start()
 
     bias_sum = jnp.zeros((2 * HEADS, 128), F32)
     for i in range(BQ):
@@ -504,8 +515,7 @@
     for c in ret:
         c.wait()
     home = home_ref[...]
-    grad_stores = []
-    for i, (ref, hbm) in enumerate(((gk, gk_hbm), (gval, gv_hbm))):
+    for i, ref in enumerate((gk, gval)):
         back = jnp.concatenate([rcv_l[i], rcv_r[i]], axis=0)
         total = acc_mid[i, RAD * CW : (RAD + CH) * CW] + dot(home, back, NN)
         gap = jnp.zeros((CELLS - RAD * CW, D), F32)
@@ -513,8 +523,6 @@
         below = down_in[i].astype(F32).reshape(RAD * CW, D)
         total = total + jnp.concatenate([above, gap], axis=0) + jnp.concatenate([gap, below], axis=0)
         ref[...] = total.astype(BF)
-        grad_stores.append(local(ref, hbm, 10 + i))
-        grad_stores[-1].start()
 
     @pl.loop(1, NZ)
     def _(k):
@@ -538,62 +546,39 @@
         b3_copy(k).wait()
         cb_copy(k).start()
 
-    def stores(of_core, first):
-        made = []
+    @pl.loop(1, GROUP)
+    def _(k):
+        bd_copy(k).wait()
+
+    ob_ref[...] = jnp.concatenate([bias_c[i, :per, : KS * KS] for i in range(GROUP)], axis=0)
+
+    @pl.loop(0, NY)
+    def _(k):
+        ca_copy(k).wait()
+        cb_copy(k).wait()
+
+
+def hand_over(*refs):
+    sources, targets, sems = refs[:5], refs[5:10], refs[10]
+    pairs = [(sources[i], targets[i]) for i in (0, 1, 2, 4)]
+    for c in range(CORES):
         for i in range(2):
             for j in range(2):
-                lanes = pl.ds(pl.multiple_of(of_core * OUTS + i * half + j * 128, 128), 128)
-                made.append(local(out.at[of_core, i, :, :, j], ow_hbm.at[:, :, :, lanes], first + 2 * i + j))
-        return made
-
-    kept = stores(core, 12)
-    for c in kept:
+                first = c * OUTS + i * OUTS // 2 + j * 128
+                pairs.append((sources[3].at[c, i, :, :, j], targets[3].at[:, :, :, first : first + 128]))
+    copies = [pltpu.make_async_copy(src, dst, sems.at[i]) for i, (src, dst) in enumerate(pairs)]
+    for c in copies:
         c.start()
-
-    @pl.loop(1, GROUP)
-    def _(k):
-        bd_copy(k).wait()
-
-    ob_ref[...] = jnp.concatenate([bias_c[i, :per, : KS * KS] for i in range(GROUP)], axis=0)
-
-    @pl.loop(0, NY)
-    def _(k):
-        ca_copy(k).wait()
-        cb_copy(k).wait()
-
-    given = stores(1 - core, 16)
-    for c in given:
-        c.start()
-    for c in (gq_store, *grad_stores, *kept, *given):
+    for c in copies:
         c.wait()
 
 
-def hand_over(*refs):
-    sources, targets, held, sems = refs[:5], refs[5:10], refs[10:15], refs[15]
-    pairs = []
-    for i in range(5):
-        chunks = range(NY) if i == 3 else (None,)
-        for c in chunks:
-            src, via, dst = (r if c is None else r.at[c] for r in (sources[i], held[i], targets[i]))
-            at_sem = len(pairs)
-            pairs.append(
-                (pltpu.make_async_copy(src, via, sems.at[0, at_sem]), pltpu.make_async_copy(via, dst, sems.at[1, at_sem]))
-            )
-    for fetch, _ in pairs:
-        fetch.start()
-    for fetch, store in pairs:
-        fetch.wait()
-        store.start()
-    for _, store in pairs:
-        store.wait()
-
-
 def on_device(queries, keys, values, grad_out, out_weight, rel_bias):
-    one_hot, places, pack, spread, join, home, heads = tables()
+    one_hot, places, pack, strip, spread, join, home, heads = tables()
     cells_out = jax.ShapeDtypeStruct((CELLS, D), BF)
     dma = pltpu.SemaphoreType.DMA
     vm = pltpu.VMEM
-    in_hbm = pl.BlockSpec(memory_space=pl.ANY)
+    in_hbm = pl.BlockSpec(memory_space=pltpu.HBM)
     in_vmem = pl.BlockSpec(memory_space=pltpu.VMEM)
     scratch = [
         vm((CH, CW, D), BF),
@@ -603,6 +588,8 @@
         vm((2, EXT, CW, D), BF),
         vm((2, 80, D), BF),
         vm((2, 80, D), BF),
+        vm((2, 64, D), BF),
+        vm((2, 64, D), BF),
         vm((2, STAGE, D), BF),
         vm((2, STAGE, D), BF),
         vm((CELLS, D), BF),
@@ -624,21 +611,17 @@
         vm((2, RAD, CW, D), BF),
         vm((2, RAD, CW, D), BF),
         vm((2, RAD, CW, D), BF),
-        vm((CELLS, D), BF),
-        vm((CELLS, D), BF),
-        vm((CELLS, D), BF),
         vm((FEATS // PROWS, PROWS, OUTS), BF),
         vm((NX, XPIECES, PROWS, OUTS), BF),
         vm((NZ, PROWS, 256), BF),
         vm((NZ, PROWS, 256), BF),
-        vm((CORES, 2, NY, NX * XPIECES, 2, PROWS, 128), BF),
         vm((GROUP, 8, 128), F32),
         vm((GROUP, 8, 128), F32),
         vm((NX, 8, 128), F32),
         vm((2, 8, 128), F32),
         vm((NZ, 8, 128), F32),
         vm((GROUP, 8, 128), F32),
-        dma((20,)),
+        dma((9,)),
     ]
     for count in (8, GROUP, (2, GROUP), 8, NX, NZ, NZ, NX, NY, NY, NX, NY, NX, GROUP, NX, NZ, GROUP):
         shape = count if isinstance(count, tuple) else (count,)
@@ -646,29 +629,35 @@
     results = pl.pallas_call(
         kernel,
         out_shape=(
+            vm((CELLS, D), BF),
+            vm((CELLS, D), BF),
+            vm((CELLS, D), BF),
+            vm((CORES, 2, NY, NX * XPIECES, 2, PROWS, 128), BF),
+            vm((HEADS, KS * KS), F32),
+        ),
+        in_specs=[in_hbm] * 5 + [in_vmem, in_hbm] + [in_vmem] * 7,
+        out_specs=(in_vmem,) * 5,
+        scratch_shapes=scratch,
+        compiler_params=pltpu.CompilerParams(
+            collective_id=0, has_side_effects=True, vmem_limit_bytes=56 * 2**20
+        ),
+        cost_estimate=pl.CostEstimate(flops=3 * 10**9, bytes_accessed=8 * 2**20, transcendentals=10**6),
+        name="attention_backward",
+    )(queries, keys, values, grad_out, out_weight, rel_bias, one_hot, places, pack, strip, spread, join, home, heads)
+    gq, gk, gv, gw, gb = pl.pallas_call(
+        hand_over,
+        out_shape=(
             cells_out,
             cells_out,
             cells_out,
             jax.ShapeDtypeStruct((NY, FEATS // PROWS, PROWS, D), BF),
             jax.ShapeDtypeStruct((HEADS, KS * KS), F32),
         ),
-        in_specs=[in_hbm] * 5 + [in_vmem, in_hbm] + [in_vmem] * 6,
-        out_specs=(in_hbm, in_hbm, in_hbm, in_hbm, in_vmem),
-        scratch_shapes=scratch,
-        compiler_params=pltpu.CompilerParams(
-            collective_id=0, has_side_effects=True, vmem_limit_bytes=56 * 2**20
-        ),
-        cost_estimate=pl.CostEstimate(flops=3 * 10**9, bytes_accessed=8 * 2**20, transcendentals=10**6),
-        name="attention_backward",
-    )(queries, keys, values, grad_out, out_weight, rel_bias, one_hot, places, pack, spread, join, home, heads)
-    gq, gk, gv, gw, gb = pl.pallas_call(
-        hand_over,
-        out_shape=tuple(jax.ShapeDtypeStruct(r.shape, r.dtype) for r in results),
-        in_specs=[in_hbm] * 5,
+        in_specs=[in_vmem] * 5,
         out_specs=(in_hbm,) * 5,
-        scratch_shapes=[vm(r.shape, r.dtype) for r in results] + [dma((2, 4 + NY))],
+        scratch_shapes=[dma((4 + 4 * CORES,))],
         name="hand_over",
-    )(*results)
+    )(*(pltpu.with_memory_space_constraint(r, pltpu.VMEM) for r in results))
     shape = queries.shape
     return gq.reshape(shape), gk.reshape(shape), gv.reshape(shape), gw.reshape(D, D), gb
 

time: 89.1 us -> 79.1 us (0.89)
  Pallas kernels: 88.3 us -> 78.4 us
    pallas_call x2, Pallas kernels: 88.3 us -> 78.4 us  [the longest x1 76.7 us: on_device(): pl.pallas_call(kernel, out_shape=(vm((CELLS, D), BF), vm((CELLS, D), BF),...]
where the time goes in v3:
time: 79.1 us; the launch traced here: 79 us
  Pallas kernels  78.4 us (99%)
    pallas_call x1, Pallas kernels, on_device(): pl.pallas_call(kernel, out_shape=(vm((CELLS, D), BF), vm((CELLS, D), BF),...  76.7 us
    pallas_call x1, Pallas kernels, on_device(): pl.pallas_call(hand_over, out_shape=(cells_out, cells_out, cells_out, jax...  1.68 us

profile of v3, /device:TPU:1, one launch (start us, length us, event | category | flops | bytes accessed | tf_op | source)
XLA Modules:
  0.0 79.0 jit_solution(17489562818340696347)
XLA Ops:
  0.6 76.7 %attention_backward.1 = (bf16[128,1024]{1,0:T(8,128)(2,1)S(1)}, bf16[128,1024]{1,0:T(8,128)(2,1)S(1)}, bf16[128,1024]{1,0:T(8,128)(2,1)S(1)}, bf16[2,2,4,16,2,16...) custom-call(bf16[16,8,1024]{2,1,0:T(8,128)(2,1)} %q_hbm.1, bf16[16,8,1024]{2,1,0:T(8,128)(2,1)} %k_hbm.1, ...), custom_call_target="tpu_custom_call" | custom-call | flops 3000000000 | bytes 8388608 | tf_op jit(solution)/shard_map/attention_backward/pallas_call | solution.py:629
  77.4 1.7 %hand_over.1 = (bf16[128,1024]{1,0:T(8,128)(2,1)}, bf16[128,1024]{1,0:T(8,128)(2,1)}, bf16[128,1024]{1,0:T(8,128)(2,1)}, bf16[4,16,16,1024]{3,2,1,0:T(8,128)(2,1)}, f32[16,121]{1,0:T(8,128)}) custom-call(bf16[128,1024]{1,0:T(8,128)(2,1)S(1)} %get-tuple-element.15.refs_0_, bf16[128,1024]{1,0:T(8,128)(2,1)S(1)} %get-tuple-element.16.refs_1_, ...), custom_call_target="tpu_custom_call" | custom-call | tf_op jit(solution)/shard_map/hand_over/pallas_call | solution.py:647

commit v4 on v3

--- a/solution.py
+++ b/solution.py
@@ -36,7 +36,7 @@
 PROWS = 16
 XPIECES = FEATS // PROWS // NX
 NEG = -1e30
-NEIGHBOURS = ((0, -1), (0, 1), (-1, 0), (1, 0), (-1, -1), (1, -1), (-1, 1), (1, 1))
+NEIGHBOURS = ((0, -1), (0, 1), (-1, 0), (1, 0))
 
 
 def key_places():
@@ -77,17 +77,12 @@
     strip[64 + corner, corner // RAD * CW + CW - RAD + corner % RAD] = True
     join = np.zeros((2 * STAGE, BLOCKS * 2 * SIDEK), bool)
     for b in range(BLOCKS):
-        place = np.arange(SIDEK)
-        join[6 + 20 * b + place, 2 * SIDEK * b + place] = True
-        join[STAGE + 6 + 20 * b + place, 2 * SIDEK * b + SIDEK + place] = True
-    entry = np.arange(STAGE)
-    cell = np.where(entry < 32, entry, np.where(entry < 112, entry - 32, entry - 64))
-    home = np.zeros((CELLS, 2 * STAGE), bool)
-    home[cell // RAD * CW + cell % RAD, entry] = True
-    home[cell // RAD * CW + CW - RAD + cell % RAD, STAGE + entry] = True
+        at = spread[b * SIDEK : (b + 1) * SIDEK].T
+        join[:STAGE, 2 * SIDEK * b : 2 * SIDEK * b + SIDEK] = at
+        join[STAGE:, 2 * SIDEK * b + SIDEK : 2 * SIDEK * (b + 1)] = at
     heads = np.repeat(np.arange(4), BQ)[:, None] == (np.arange(256) // 64)[None, :]
     as_low = lambda t: np.asarray(t, np.float32).astype(jnp.bfloat16)
-    return (as_low(one_hot), places, as_low(pack), as_low(strip), as_low(spread), as_low(join), as_low(home), as_low(heads))
+    return (as_low(one_hot), places, as_low(pack), as_low(strip), as_low(spread), as_low(join), as_low(heads))
 
 
 def dot(a, b, dims):
@@ -100,7 +95,7 @@
 
 
 def kernel(
-    q_hbm, k_hbm, v_hbm, g_hbm, w_hbm, bias_ref, oh_hbm, places_ref, pack_ref, strip_ref, spread_ref, join_ref, home_ref, heads_ref,
+    q_hbm, k_hbm, v_hbm, g_hbm, w_hbm, bias_ref, oh_hbm, places_ref, pack_ref, strip_ref, spread_ref, join_ref, heads_ref,
     gq, gk, gval, out, ob_ref,
     qv, gv, wv, ohv, mid, panel_l, panel_r, strip_l, strip_r, stage_l, stage_r, ga, kb, vb, table, probs, att, at, go,
     sg_sum, acc_mid, side, ret_l, ret_r, rcv_l, rcv_r, up_out, down_out, up_in, down_in,
@@ -347,21 +342,17 @@
         joined = dot(join_ref[...], side[i], NN).astype(BF)
         ret_l[i] = joined[:STAGE]
         ret_r[i] = joined[STAGE:]
-    up_out[...] = acc_mid[:, : RAD * CW].reshape(2, RAD, CW, D).astype(BF)
-    down_out[...] = acc_mid[:, (RAD + CH) * CW :].reshape(2, RAD, CW, D).astype(BF)
     ret_parts = (
-        (ret_l.at[:, 32:112], rcv_r.at[:, 32:112]),
-        (ret_r.at[:, 32:112], rcv_l.at[:, 32:112]),
-        (up_out, down_in),
-        (down_out, up_in),
-        (ret_l.at[:, 0:32], rcv_r.at[:, 112:144]),
-        (ret_l.at[:, 112:144], rcv_r.at[:, 0:32]),
-        (ret_r.at[:, 0:32], rcv_l.at[:, 112:144]),
-        (ret_r.at[:, 112:144], rcv_l.at[:, 0:32]),
+        (ret_l.at[:, 80:], rcv_r.at[:, 80:], 0),
+        (ret_r.at[:, 80:], rcv_l.at[:, 80:], 1),
+        (ret_l.at[:, :80], rcv_r.at[:, :80], 0),
+        (ret_r.at[:, :80], rcv_l.at[:, :80], 1),
+        (up_out, down_in, 2),
+        (down_out, up_in, 3),
     )
     ret = [
-        remote(src, dst, ret_ss.at[i], ret_rs.at[i], neighbour(*NEIGHBOURS[i]))
-        for i, (src, dst) in enumerate(ret_parts)
+        remote(src, dst, ret_ss.at[i], ret_rs.at[i], neighbour(*NEIGHBOURS[n]))
+        for i, (src, dst, n) in enumerate(ret_parts)
     ]
 
     rx_own.wait()
@@ -384,8 +375,27 @@
     def _(k):
         rz_copy(k).start()
 
-    for c in ret:
+    for c in ret[:4]:
         c.start()
+
+    rz[0] = wz[z]
+
+    @pl.loop(1, NZ)
+    def _(k):
+        rz_copy(k).wait()
+
+    final = jnp.sum(rz[...].astype(F32), axis=0).astype(BF)
+    spot = x * XPIECES + z // 2
+    out[core, 0, y, spot, z % 2] = final[:, :128]
+    out[core, 1, y, spot, z % 2] = final[:, 128:]
+    mine = out.at[core, :, y, spot, z % 2]
+
+    def zg_copy(k):
+        return remote(mine, mine, zg_ss.at[k], zg_rs.at[k], along_z(k))
+
+    @pl.loop(1, NZ)
+    def _(k):
+        zg_copy(k).start()
 
     bias_sum = jnp.zeros((2 * HEADS, 128), F32)
     for i in range(BQ):
@@ -407,24 +417,37 @@
     def _(k):
         ba_copy(k).start()
 
-    rz[0] = wz[z]
-
     @pl.loop(1, NZ)
     def _(k):
-        rz_copy(k).wait()
-
-    final = jnp.sum(rz[...].astype(F32), axis=0).astype(BF)
-    spot = x * XPIECES + z // 2
-    out[core, 0, y, spot, z % 2] = final[:, :128]
-    out[core, 1, y, spot, z % 2] = final[:, 128:]
-    mine = out.at[core, :, y, spot, z % 2]
-
-    def zg_copy(k):
-        return remote(mine, mine, zg_ss.at[k], zg_rs.at[k], along_z(k))
-
-    @pl.loop(1, NZ)
-    def _(k):
-        zg_copy(k).start()
+        zg_copy(k).wait()
+
+    slab_a = out.at[core, 0, y, pl.ds(x * XPIECES, XPIECES)]
+    slab_b = out.at[core, 1, y, pl.ds(x * XPIECES, XPIECES)]
+
+    def a2_copy(k):
+        return remote(slab_a, slab_a, a2_ss.at[k], a2_rs.at[k], along_x(k))
+
+    def b2_copy(k):
+        return remote(slab_b, slab_b, b2_ss.at[k], b2_rs.at[k], along_y(k))
+
+    @pl.loop(1, NX)
+    def _(k):
+        a2_copy(k).start()
+
+    @pl.loop(1, NY)
+    def _(k):
+        b2_copy(k).start()
+
+    ret[0].wait()
+    ret[1].wait()
+    for i in range(2):
+        back = jnp.concatenate([rcv_l[i, 80:], rcv_r[i, 80:]], axis=0)
+        corners = dot(strip_ref[...], back, TN)
+        rim = RAD * CW
+        up_out[i] = (acc_mid[i, :rim] + corners[:rim]).reshape(RAD, CW, D).astype(BF)
+        down_out[i] = (acc_mid[i, rim + CELLS :] + corners[rim:]).reshape(RAD, CW, D).astype(BF)
+    ret[4].start()
+    ret[5].start()
 
     @pl.loop(1, GROUP)
     def _(k):
@@ -443,26 +466,42 @@
     def _(k):
         bx_copy(k).start()
 
-    @pl.loop(1, NZ)
-    def _(k):
-        zg_copy(k).wait()
-
-    slab_a = out.at[core, 0, y, pl.ds(x * XPIECES, XPIECES)]
-    slab_b = out.at[core, 1, y, pl.ds(x * XPIECES, XPIECES)]
-
-    def a2_copy(k):
-        return remote(slab_a, slab_a, a2_ss.at[k], a2_rs.at[k], along_x(k))
-
-    def b2_copy(k):
-        return remote(slab_b, slab_b, b2_ss.at[k], b2_rs.at[k], along_y(k))
-
-    @pl.loop(1, NX)
-    def _(k):
-        a2_copy(k).start()
+    def part_a(k):
+        return out.at[core, 0, (y + k + NY) % NY]
+
+    def part_b(k):
+        return out.at[core, 1, :, pl.ds((x + k + NX) % NX * XPIECES, XPIECES)]
+
+    def a3_copy(k):
+        return remote(part_a(0), part_a(0), a3_ss.at[k], a3_rs.at[k], along_y(k))
+
+    def b3_copy(k):
+        return remote(part_b(0), part_b(0), b3_ss.at[k], b3_rs.at[k], along_x(k))
+
+    def ca_copy(k):
+        return remote(part_a(-k), part_a(-k), ca_ss.at[k], ca_rs.at[k], device(x, y, z, 1 - core))
+
+    def cb_copy(k):
+        return remote(part_b(-k), part_b(-k), cb_ss.at[k], cb_rs.at[k], device(x, y, z, 1 - core))
+
+    @pl.loop(1, NX)
+    def _(k):
+        a2_copy(k).wait()
 
     @pl.loop(1, NY)
     def _(k):
-        b2_copy(k).start()
+        a3_copy(k).start()
+
+    @pl.loop(1, NY)
+    def _(k):
+        b2_copy(k).wait()
+
+    @pl.loop(1, NX)
+    def _(k):
+        b3_copy(k).start()
+
+    ca_copy(0).start()
+    cb_copy(0).start()
 
     @pl.loop(1, NX)
     def _(k):
@@ -475,69 +514,31 @@
     def _(k):
         bz_copy(k).start()
 
-    def part_a(k):
-        return out.at[core, 0, (y + k + NY) % NY]
-
-    def part_b(k):
-        return out.at[core, 1, :, pl.ds((x + k + NX) % NX * XPIECES, XPIECES)]
-
-    def a3_copy(k):
-        return remote(part_a(0), part_a(0), a3_ss.at[k], a3_rs.at[k], along_y(k))
-
-    def b3_copy(k):
-        return remote(part_b(0), part_b(0), b3_ss.at[k], b3_rs.at[k], along_x(k))
-
-    def ca_copy(k):
-        return remote(part_a(-k), part_a(-k), ca_ss.at[k], ca_rs.at[k], device(x, y, z, 1 - core))
-
-    def cb_copy(k):
-        return remote(part_b(-k), part_b(-k), cb_ss.at[k], cb_rs.at[k], device(x, y, z, 1 - core))
-
-    @pl.loop(1, NX)
-    def _(k):
-        a2_copy(k).wait()
-
-    @pl.loop(1, NY)
-    def _(k):
-        a3_copy(k).start()
-
-    @pl.loop(1, NY)
-    def _(k):
-        b2_copy(k).wait()
-
-    @pl.loop(1, NX)
-    def _(k):
-        b3_copy(k).start()
-
-    ca_copy(0).start()
-    cb_copy(0).start()
-
-    for c in ret:
+    @pl.loop(1, NZ)
+    def _(k):
+        bz_copy(k).wait()
+
+    bias_zin[0] = bias_b[1]
+    bias_c[me_group] = jnp.sum(bias_zin[...], axis=0)
+    bias_mine = bias_c.at[me_group]
+
+    def bd_copy(k):
+        return remote(bias_mine, bias_mine, bd_ss.at[k], bd_rs.at[k], member(k)[2])
+
+    @pl.loop(1, GROUP)
+    def _(k):
+        bd_copy(k).start()
+
+    for c in ret[2:]:
         c.wait()
-    home = home_ref[...]
     for i, ref in enumerate((gk, gval)):
-        back = jnp.concatenate([rcv_l[i], rcv_r[i]], axis=0)
-        total = acc_mid[i, RAD * CW : (RAD + CH) * CW] + dot(home, back, NN)
+        back = jnp.concatenate([rcv_l[i, :80], rcv_r[i, :80]], axis=0)
+        total = acc_mid[i, RAD * CW : (RAD + CH) * CW] + dot(pack_ref[...], back, TN)
         gap = jnp.zeros((CELLS - RAD * CW, D), F32)
         above = up_in[i].astype(F32).reshape(RAD * CW, D)
         below = down_in[i].astype(F32).reshape(RAD * CW, D)
         total = total + jnp.concatenate([above, gap], axis=0) + jnp.concatenate([gap, below], axis=0)
         ref[...] = total.astype(BF)
-
-    @pl.loop(1, NZ)
-    def _(k):
-        bz_copy(k).wait()
-
-    bias_zin[0] = bias_b[1]
-    bias_c[me_group] = jnp.sum(bias_zin[...], axis=0)
-    bias_mine = bias_c.at[me_group]
-
-    def bd_copy(k):
-        return remote(bias_mine, bias_mine, bd_ss.at[k], bd_rs.at[k], member(k)[2])
-
-    @pl.loop(1, GROUP)
-    def _(k):
-        bd_copy(k).start()
 
     @pl.loop(1, NY)
     def _(k):
@@ -574,7 +575,7 @@
 
 
 def on_device(queries, keys, values, grad_out, out_weight, rel_bias):
-    one_hot, places, pack, strip, spread, join, home, heads = tables()
+    one_hot, places, pack, strip, spread, join, heads = tables()
     cells_out = jax.ShapeDtypeStruct((CELLS, D), BF)
     dma = pltpu.SemaphoreType.DMA
     vm = pltpu.VMEM
@@ -623,7 +624,7 @@
         vm((GROUP, 8, 128), F32),
         dma((9,)),
     ]
-    for count in (8, GROUP, (2, GROUP), 8, NX, NZ, NZ, NX, NY, NY, NX, NY, NX, GROUP, NX, NZ, GROUP):
+    for count in (6, GROUP, (2, GROUP), 6, NX, NZ, NZ, NX, NY, NY, NX, NY, NX, GROUP, NX, NZ, GROUP):
         shape = count if isinstance(count, tuple) else (count,)
         scratch += [dma(shape), dma(shape)]
     results = pl.pallas_call(
@@ -635,7 +636,7 @@
             vm((CORES, 2, NY, NX * XPIECES, 2, PROWS, 128), BF),
             vm((HEADS, KS * KS), F32),
         ),
-        in_specs=[in_hbm] * 5 + [in_vmem, in_hbm] + [in_vmem] * 7,
+        in_specs=[in_hbm] * 5 + [in_vmem, in_hbm] + [in_vmem] * 6,
         out_specs=(in_vmem,) * 5,
         scratch_shapes=scratch,
         compiler_params=pltpu.CompilerParams(
@@ -643,7 +644,7 @@
         ),
         cost_estimate=pl.CostEstimate(flops=3 * 10**9, bytes_accessed=8 * 2**20, transcendentals=10**6),
         name="attention_backward",
-    )(queries, keys, values, grad_out, out_weight, rel_bias, one_hot, places, pack, strip, spread, join, home, heads)
+    )(queries, keys, values, grad_out, out_weight, rel_bias, one_hot, places, pack, strip, spread, join, heads)
     gq, gk, gv, gw, gb = pl.pallas_call(
         hand_over,
         out_shape=(

time: 79.1 us -> 77.3 us (0.977)
  Pallas kernels: 78.4 us -> 76.6 us
    pallas_call x1, Pallas kernels: 76.7 us -> 74.9 us  [on_device(): pl.pallas_call(kernel, out_shape=(vm((CELLS, D), BF), vm((CELLS, D), BF),...]
where the time goes in v4:
time: 77.3 us; the launch traced here: 77.2 us
  Pallas kernels  76.6 us (99%)
    pallas_call x1, Pallas kernels, on_device(): pl.pallas_call(kernel, out_shape=(vm((CELLS, D), BF), vm((CELLS, D), BF),...  74.9 us
    pallas_call x1, Pallas kernels, on_device(): pl.pallas_call(hand_over, out_shape=(cells_out, cells_out, cells_out, jax...  1.68 us

profile of v4, /device:TPU:1, one launch (start us, length us, event | category | flops | bytes accessed | tf_op | source)
XLA Modules:
  0.0 77.2 jit_solution(4592906062416214091)
XLA Ops:
  0.6 74.9 %attention_backward.1 = (bf16[128,1024]{1,0:T(8,128)(2,1)S(1)}, bf16[128,1024]{1,0:T(8,128)(2,1)S(1)}, bf16[128,1024]{1,0:T(8,128)(2,1)S(1)}, bf16[2,2,4,16,2,16...) custom-call(bf16[16,8,1024]{2,1,0:T(8,128)(2,1)} %q_hbm.1, bf16[16,8,1024]{2,1,0:T(8,128)(2,1)} %k_hbm.1, ...), custom_call_target="tpu_custom_call" | custom-call | flops 3000000000 | bytes 8388608 | tf_op jit(solution)/shard_map/attention_backward/pallas_call | solution.py:630
  75.6 1.7 %hand_over.1 = (bf16[128,1024]{1,0:T(8,128)(2,1)}, bf16[128,1024]{1,0:T(8,128)(2,1)}, bf16[128,1024]{1,0:T(8,128)(2,1)}, bf16[4,16,16,1024]{3,2,1,0:T(8,128)(2,1)}, f32[16,121]{1,0:T(8,128)}) custom-call(bf16[128,1024]{1,0:T(8,128)(2,1)S(1)} %get-tuple-element.15.refs_0_, bf16[128,1024]{1,0:T(8,128)(2,1)S(1)} %get-tuple-element.16.refs_1_, ...), custom_call_target="tpu_custom_call" | custom-call | tf_op jit(solution)/shard_map/hand_over/pallas_call | solution.py:648

commit v5 on v4

--- a/solution.py
+++ b/solution.py
@@ -430,13 +430,13 @@
     def b2_copy(k):
         return remote(slab_b, slab_b, b2_ss.at[k], b2_rs.at[k], along_y(k))
 
+    @pl.loop(1, NY)
+    def _(k):
+        b2_copy(k).start()
+
     @pl.loop(1, NX)
     def _(k):
         a2_copy(k).start()
-
-    @pl.loop(1, NY)
-    def _(k):
-        b2_copy(k).start()
 
     ret[0].wait()
     ret[1].wait()
@@ -490,7 +490,7 @@
 
     @pl.loop(1, NY)
     def _(k):
-        a3_copy(k).start()
+        a3_copy(1 + k % (NY - 1)).start()
 
     @pl.loop(1, NY)
     def _(k):
@@ -498,7 +498,7 @@
 
     @pl.loop(1, NX)
     def _(k):
-        b3_copy(k).start()
+        b3_copy(1 + k % (NX - 1)).start()
 
     ca_copy(0).start()
     cb_copy(0).start()

time: 77.3 us -> 77.3 us (level)
  no operation moved by 1% of the time
where the time goes in v5:
time: 77.3 us; the launch traced here: 77.2 us
  Pallas kernels  76.6 us (99%)
    pallas_call x1, Pallas kernels, on_device(): pl.pallas_call(kernel, out_shape=(vm((CELLS, D), BF), vm((CELLS, D), BF),...  74.9 us
    pallas_call x1, Pallas kernels, on_device(): pl.pallas_call(hand_over, out_shape=(cells_out, cells_out, cells_out, jax...  1.68 us

profile of v5, /device:TPU:1, one launch (start us, length us, event | category | flops | bytes accessed | tf_op | source)
XLA Modules:
  0.0 77.2 jit_solution(12543761332760467477)
XLA Ops:
  0.6 74.9 %attention_backward.1 = (bf16[128,1024]{1,0:T(8,128)(2,1)S(1)}, bf16[128,1024]{1,0:T(8,128)(2,1)S(1)}, bf16[128,1024]{1,0:T(8,128)(2,1)S(1)}, bf16[2,2,4,16,2,16...) custom-call(bf16[16,8,1024]{2,1,0:T(8,128)(2,1)} %q_hbm.1, bf16[16,8,1024]{2,1,0:T(8,128)(2,1)} %k_hbm.1, ...), custom_call_target="tpu_custom_call" | custom-call | flops 3000000000 | bytes 8388608 | tf_op jit(solution)/shard_map/attention_backward/pallas_call | solution.py:630
  75.5 1.7 %hand_over.1 = (bf16[128,1024]{1,0:T(8,128)(2,1)}, bf16[128,1024]{1,0:T(8,128)(2,1)}, bf16[128,1024]{1,0:T(8,128)(2,1)}, bf16[4,16,16,1024]{3,2,1,0:T(8,128)(2,1)}, f32[16,121]{1,0:T(8,128)}) custom-call(bf16[128,1024]{1,0:T(8,128)(2,1)S(1)} %get-tuple-element.15.refs_0_, bf16[128,1024]{1,0:T(8,128)(2,1)S(1)} %get-tuple-element.16.refs_1_, ...), custom_call_target="tpu_custom_call" | custom-call | tf_op jit(solution)/shard_map/hand_over/pallas_call | solution.py:648
